TPU v7x, 32 devices: a whole 2x2x4 slice. The times are simulated.
32 devices in a mesh: seq: 8 (over z, y), head: 4 (over x, core).
Axes of the slice: x: 2, y: 2, z: 4, core: 2. Of those that a mesh axis runs over, the one named last changes fastest.
Arguments:
- x_heads: bfloat16 [4096, 32768], P(('head', 'seq')), may hold values from -6 to 6
- b_proj: bfloat16 [32768, 128], P(('seq', 'head')), may hold values from -0.5 to 0.5
- c_proj: bfloat16 [32768, 128], P(('seq', 'head')), may hold values from -6 to 6
- log_gate: float32 [64, 32768], P('head', 'seq'), may hold values from -3 to 0, as said below
- step_size: float32 [64, 32768], P('head', 'seq'), may hold values from 0.003 to 0.03
- level_weight: float32 [64, 8, 32768], P('head', None, 'seq'), may hold values from 0.25 to 4
- skip: float32 [64], P('head'), may hold values from 0.5 to 1.5
Outputs:
- y_heads: bfloat16 [4096, 32768], P(('head', 'seq'))
Inputs may be any that keep to these rules, and one draw needn't show every extreme that they name: log_gate holds no positive values.
All inputs are finite; a program needn't handle non-finite values.
Results may differ from a plain program's by a relative error of at most 0.0064.
Values may be sent and summed in bfloat16 or wider, within the bound.
No kernel may reach another device: no remote copies, remote signals or barrier semaphores. Data moves between devices by JAX's collectives and lax.ppermute only.
A program may use at most 192 MiB of HBM per device.

v0:
```python
import functools
import math

import jax
import jax.numpy as jnp
from jax import lax
from jax.experimental import pallas as pl
from jax.experimental.pallas import tpu as pltpu
from jax.sharding import PartitionSpec as P

P_SIZE = 64
N = 128
Q = 256
HALF = Q // 2
CORES = 2
NEVER = -1e30
VMEM_LIMIT = 60 * 1024 * 1024

f32 = jnp.float32
bf16 = jnp.bfloat16


def dot(a, b):
    return lax.dot_general(a, b, (((1,), (0,)), ((), ())), preferred_element_type=f32)


def exact_parts(value):
    high = value.astype(bf16)
    rest = value - high.astype(f32)
    middle = rest.astype(bf16)
    low = (rest - middle.astype(f32)).astype(bf16)
    return high, middle, low


def gates_kernel(heads, levels, padded, gates_ref, weight_ref, cum_ref, offset_ref, decay_ref, merge_ref,
                 log_scratch):
    shards, _, span_rows, _ = gates_ref.shape
    spans = shards * span_rows
    upper = (
        lax.broadcasted_iota(jnp.int32, (Q, Q), 0) <= lax.broadcasted_iota(jnp.int32, (Q, Q), 1)
    ).astype(f32).astype(bf16)
    chunk = min(spans, 64)
    for head in range(heads):
        for shard in range(shards):
            rows = pl.ds(shard * span_rows, span_rows)
            gate = gates_ref[shard, 2 * head]
            step = gates_ref[shard, 2 * head + 1]
            high, middle, low = exact_parts(gate)
            cumulative = dot(high, upper) + dot(middle, upper) + dot(low, upper)
            span_log = cumulative[:, Q - 1 :]
            cum_ref[head, rows, :] = cumulative
            offset_ref[head, rows, :] = cumulative - jnp.log(step)
            weight_ref[head, rows, :] = jnp.exp(span_log - cumulative) * step
            log_scratch[rows, :] = jnp.broadcast_to(span_log, (span_rows, N))
        high, middle, low = exact_parts(log_scratch[...])

        def some_spans(at, carry):
            first = at * chunk
            size = (chunk * padded, spans)
            row = lax.broadcasted_iota(jnp.int32, size, 0)
            span = first + row // padded
            level = row % padded
            other = lax.broadcasted_iota(jnp.int32, size, 1)
            out_rows = pl.ds(pl.multiple_of(first * padded, chunk * padded), chunk * padded)
            bit = jnp.maximum(level - 1, 0)
            before = (other >= (span >> bit) << bit) & (other < span)
            before = before.astype(f32).astype(bf16)
            decay = dot(before, high) + dot(before, middle) + dot(before, low)
            has_bit = ((span >> bit) & 1)[:, :1] == 1
            decay_ref[head, out_rows, :] = jnp.where(has_bit, decay, NEVER)
            right = (other > span - (1 << bit)) & (other <= span)
            right = right.astype(f32).astype(bf16)
            merge_ref[head, out_rows, :] = jnp.exp(
                dot(right, high) + dot(right, middle) + dot(right, low)
            )
            return carry

        lax.fori_loop(0, spans // chunk, some_spans, 0)


def pick(core, mine_ref, other_ref, local, group):
    half = group // CORES
    rows = slice(local % half * Q, (local % half + 1) * Q)
    return jnp.where(core == local // half, mine_ref[rows, :], other_ref[rows, :])


def merge_blocks(left, right, merge_ref, row, width):
    parts = []
    for head in range(merge_ref.shape[0]):
        rows = slice(head * width, (head + 1) * width)
        parts.append(left[rows] * merge_ref[head, row : row + 1, :] + right[rows])
    return jnp.concatenate(parts, axis=0) if len(parts) > 1 else parts[0]


def states_kernel(heads, width, group, padded, groups_ref, core_ref, x_ref, mine_ref, other_ref, weight_ref,
                  merge_ref, low_ref, total_ref):
    kept = {}
    for local in range(group):
        columns = slice(local * Q, (local + 1) * Q)
        parts = [
            (
                x_ref[head * width : (head + 1) * width, columns].astype(f32)
                * weight_ref[head, local : local + 1, :]
            ).astype(bf16)
            for head in range(heads)
        ]
        weighted = jnp.concatenate(parts, axis=0) if heads > 1 else parts[0]
        state = dot(weighted, pick(core_ref[0], mine_ref, other_ref, local, group))
        bit = 0
        while local >> bit & 1:
            state = merge_blocks(kept[bit], state, merge_ref, local * padded + bit + 1, width)
            bit += 1
        kept[bit] = state
        if local < group - 1:
            low_ref[local] = state.astype(bf16)
    total_ref[...] = state


def tree_kernel(width, group, padded, groups_ref, merge_ref, *refs):
    *total_refs, high_ref, order_ref = refs
    steps = order_ref.shape[0]
    low_bits = group.bit_length() - 1
    at = 0
    for total_ref in total_refs:
        for slot in range(total_ref.shape[0]):
            order_ref[groups_ref[at]] = total_ref[slot]
            at += 1
    kept = {}
    for step in range(steps):
        state = order_ref[step]
        bit = 0
        while step >> bit & 1:
            row = ((step + 1) * group - 1) * padded + low_bits + bit + 1
            state = merge_blocks(kept[bit], state, merge_ref, row, width)
            bit += 1
        kept[bit] = state
        high_ref[step] = state.astype(bf16)


def outputs_kernel(heads, width, group, bits, padded, groups_ref, core_ref, skip_ref, x_ref, my_key_ref,
                   other_key_ref, my_query_ref, other_query_ref, low_ref, high_ref, cum_ref, offset_ref, decay_ref,
                   level_ref, *refs):
    out_ref, query_ref, score_ref, mixing_ref = refs[-4:]
    step = groups_ref[pl.program_id(0)]
    low_bits = group.bit_length() - 1
    levels = bits + 1
    causal = lax.broadcasted_iota(jnp.int32, (HALF, HALF), 0) <= lax.broadcasted_iota(
        jnp.int32, (HALF, HALF), 1
    )
    head_rows = [slice(head * width, (head + 1) * width) for head in range(heads)]
    high_slots = [
        jnp.maximum((step >> (bit - low_bits) << (bit - low_bits)) - 1, 0) for bit in range(low_bits, bits)
    ]
    offsets = [jnp.transpose(offset_ref[head]) for head in range(heads)]

    @pl.when(pl.program_id(0) == 0)
    def _():
        mixing_ref[:, :, HALF:, :HALF] = jnp.zeros((2, heads, HALF, HALF), bf16)

    def span_columns(local):
        return slice(local * Q, (local + 1) * Q)

    def score(local):
        slot = local % 2
        query_ref[slot] = jnp.transpose(pick(core_ref[0], my_query_ref, other_query_ref, local, group))
        keys = pick(core_ref[0], my_key_ref, other_key_ref, local, group)
        upper = dot(keys[:HALF], query_ref[slot])
        score_ref[slot, :HALF, :HALF] = jnp.where(causal, upper[:, :HALF], 0.0)
        score_ref[slot, :HALF, HALF:] = upper[:, HALF:]
        lower = dot(keys[HALF:], query_ref[slot, :, HALF:])
        score_ref[slot, HALF:, HALF:] = jnp.where(causal, lower, 0.0)

    def mix(local):
        slot = local % 2
        for head in range(heads):
            left = cum_ref[head, local : local + 1, :HALF]
            right = cum_ref[head, local : local + 1, HALF:]
            column = offsets[head][:, local : local + 1]
            upper = jnp.broadcast_to(column[:HALF], (HALF, HALF))
            lower = jnp.broadcast_to(column[HALF:], (HALF, HALF))
            mixing_ref[slot, head, :HALF, :HALF] = (
                score_ref[slot, :HALF, :HALF] * jnp.exp(jnp.minimum(left - upper, 64.0))
            ).astype(bf16)
            mixing_ref[slot, head, :HALF, HALF:] = (
                score_ref[slot, :HALF, HALF:] * jnp.exp(right - upper)
            ).astype(bf16)
            mixing_ref[slot, head, HALF:, HALF:] = (
                score_ref[slot, HALF:, HALF:] * jnp.exp(jnp.minimum(right - lower, 64.0))
            ).astype(bf16)

    def level_parts(local):
        slot = local % 2
        columns = span_columns(local)
        weights = level_ref[0, :, columns].astype(f32)
        factors = []
        for head in range(heads):
            decay = decay_ref[head, local * padded : local * padded + levels, :]
            decay = jnp.concatenate([decay] * (Q // N), axis=1)
            growth = jnp.exp(cum_ref[head, local : local + 1, :] + decay)
            factors.append(weights[head * levels : (head + 1) * levels] * growth)
        sums = [None] * heads
        for bit in range(bits):
            if bit < low_bits:
                if not local >> bit & 1:
                    continue
                state = low_ref[((local >> bit) << bit) - 1]
            else:
                state = high_ref[high_slots[bit - low_bits]]
            part = dot(state, query_ref[slot])
            for head in range(heads):
                term = part[head_rows[head]] * factors[head][bit + 1 : bit + 2]
                sums[head] = term if sums[head] is None else sums[head] + term
        return sums, [weights[head * levels : head * levels + 1] for head in range(heads)]

    def finish(local, parts):
        slot = local % 2
        columns = span_columns(local)
        sums, own = parts
        for head in range(heads):
            values = x_ref[head_rows[head], columns]
            result = dot(values, mixing_ref[slot, head]) * own[head] + skip_ref[head] * values.astype(f32)
            if sums[head] is not None:
                result += sums[head]
            out_ref[head_rows[head], columns] = result.astype(bf16)

    score(0)
    for local in range(group):
        parts = level_parts(local)
        if local + 1 < group:
            score(local + 1)
        mix(local)
        finish(local, parts)


def exchange(value, axis, distance):
    pairs = [(place, place ^ distance) for place in range(lax.axis_size(axis))]
    return lax.ppermute(value, axis, pairs)


def along_z(own):
    pieces = [own]
    for distance in range(1, lax.axis_size("z")):
        low = distance & -distance
        pieces.append(exchange(pieces[distance ^ low], "z", low))
    return jnp.concatenate(pieces, axis=0)


def in_plane(piece):
    half = piece.shape[0] // 2
    far = {}
    for distance in range(1, lax.axis_size("x")):
        far[0, distance] = exchange(piece, "x", distance)
    for distance in range(1, lax.axis_size("y")):
        far[distance, 0] = exchange(piece, "y", distance)
    for y in range(1, lax.axis_size("y")):
        for x in range(1, lax.axis_size("x")):
            first = exchange(far[0, x][:half], "y", y)
            second = exchange(far[y, 0][half:], "x", x)
            far[y, x] = jnp.concatenate([first, second], axis=0)
    return {(0, 0): piece, **far}


def both_cores(plane):
    return {place: (piece, exchange(piece, "core", 1)) for place, piece in plane.items()}


def after(value, *others):
    return lax.optimization_barrier((value, *others))[0]


def on_device(x_heads, b_proj, c_proj, log_gate, step_size, level_weight, skip):
    rows, tokens = x_heads.shape
    head_count, tok_dev = log_gate.shape
    levels = level_weight.shape[1]
    bits = levels - 1
    shards = lax.axis_size(("z", "y"))
    span_rows = tok_dev // Q
    spans = tokens // Q
    heads = max(rows // P_SIZE, 1)
    width = rows // heads
    sharing = P_SIZE // width
    block = b_proj.shape[0]
    group = CORES * block // Q
    padded = -(-levels // 8) * 8
    steps = spans // group
    per_shard = span_rows // group

    def to_owners(value):
        value = jnp.repeat(value, sharing, axis=0) if sharing > 1 else value
        value = value.reshape((shards, heads) + value.shape[1:])
        return value.reshape((shards, -1) + value.shape[3:])

    gates = jnp.stack(
        [log_gate.reshape(head_count, span_rows, Q), step_size.reshape(head_count, span_rows, Q)], axis=1
    )
    gates = lax.all_to_all(to_owners(gates), ("z", "y"), split_axis=0, concat_axis=0, tiled=True)
    key_line = along_z(b_proj)
    level_rows = lax.all_to_all(
        to_owners(after(level_weight, gates).astype(bf16)), ("z", "y"), split_axis=0, concat_axis=0, tiled=True
    )
    key_sets = both_cores(in_plane(key_line))
    query_sets = both_cores(in_plane(along_z(after(c_proj, key_line, gates))))
    first_head = lax.axis_index(("z", "y")) * rows // P_SIZE
    own_skip = lax.dynamic_slice_in_dim(skip, first_head, heads, 0)
    core = lax.axis_index("core").astype(jnp.int32).reshape(1)

    def group_ids(place):
        z = lax.axis_index("z") ^ jnp.arange(lax.axis_size("z"))
        y = lax.axis_index("y") ^ place[0]
        x = lax.axis_index("x") ^ place[1]
        return ((z * lax.axis_size("y") + y) * lax.axis_size("x") + x).astype(jnp.int32)

    params = pltpu.CompilerParams(vmem_limit_bytes=VMEM_LIMIT)
    weight, cumulative, offset, decay, merge = pl.pallas_call(
        functools.partial(gates_kernel, heads, levels, padded),
        out_shape=[jax.ShapeDtypeStruct((heads, spans, Q), f32)] * 3
        + [jax.ShapeDtypeStruct((heads, spans * padded, N), f32)] * 2,
        scratch_shapes=[pltpu.VMEM((spans, N), f32)],
        compiler_params=params,
        name="gates",
    )(gates)
    weight, cumulative, offset = [v.reshape(heads, steps, group, Q) for v in (weight, cumulative, offset)]

    x_spec = pl.BlockSpec((rows, group * Q), lambda i, ids, *_: (0, ids[i]))
    token_spec = pl.BlockSpec((block, N), lambda i, *_: (i, 0))
    span_spec = pl.BlockSpec((heads, None, group, Q), lambda i, ids, *_: (0, ids[i], 0, 0))
    level_spec = pl.BlockSpec((heads, group * padded, N), lambda i, ids, *_: (0, ids[i], 0))
    low_slots = max(group - 1, 1)
    low_spec = pl.BlockSpec((None, low_slots, rows, N), lambda i, *_: (i, 0, 0, 0))

    sets = [
        (group_ids(place), key_sets[place], query_sets[place])
        for place in sorted(key_sets, key=lambda place: ((place[0] > 0) + (place[1] > 0), place))
    ]
    lows, totals = [], []
    for ids, keys, _ in sets:
        count = ids.shape[0]
        low, total = pl.pallas_call(
            functools.partial(states_kernel, heads, width, group, padded),
            grid_spec=pltpu.PrefetchScalarGridSpec(
                num_scalar_prefetch=2,
                grid=(count,),
                in_specs=[x_spec, token_spec, token_spec, span_spec, level_spec],
                out_specs=[low_spec, pl.BlockSpec((None, rows, N), lambda i, *_: (i, 0, 0))],
            ),
            out_shape=[
                jax.ShapeDtypeStruct((count, low_slots, rows, N), bf16),
                jax.ShapeDtypeStruct((count, rows, N), f32),
            ],
            compiler_params=params,
            cost_estimate=pl.CostEstimate(
                flops=2 * rows * count * group * Q * N,
                bytes_accessed=4 * count * group * Q * (rows + N),
                transcendentals=0,
            ),
            name="states",
        )(ids, core, x_heads, *keys, weight, merge)
        lows.append(low)
        totals.append(total)

    vmem = pl.BlockSpec(memory_space=pltpu.VMEM)
    high = pl.pallas_call(
        functools.partial(tree_kernel, width, group, padded),
        grid_spec=pltpu.PrefetchScalarGridSpec(
            num_scalar_prefetch=1,
            in_specs=[vmem] * (1 + len(totals)),
            out_specs=vmem,
            scratch_shapes=[pltpu.VMEM((steps, rows, N), f32)],
        ),
        out_shape=jax.ShapeDtypeStruct((steps, rows, N), bf16),
        compiler_params=params,
        name="tree",
    )(jnp.concatenate([ids for ids, _, _ in sets]), merge, *totals)

    out = None
    for (ids, keys, queries), low in zip(sets, lows):
        count = ids.shape[0]
        tokens_here = count * group * Q
        before = [] if out is None else [out]
        out = pl.pallas_call(
            functools.partial(outputs_kernel, heads, width, group, bits, padded),
            grid_spec=pltpu.PrefetchScalarGridSpec(
                num_scalar_prefetch=2,
                grid=(count,),
                in_specs=[
                    pl.BlockSpec(memory_space=pltpu.SMEM),
                    x_spec,
                    token_spec,
                    token_spec,
                    token_spec,
                    token_spec,
                    low_spec,
                    vmem,
                    span_spec,
                    span_spec,
                    level_spec,
                    pl.BlockSpec(
                        (1, heads * levels, group * Q),
                        lambda i, ids, *_: (ids[i] // per_shard, 0, ids[i] % per_shard),
                    ),
                ]
                + [pl.BlockSpec(memory_space=pl.ANY)] * len(before),
                out_specs=x_spec,
                scratch_shapes=[
                    pltpu.VMEM((2, N, Q), bf16),
                    pltpu.VMEM((2, Q, Q), f32),
                    pltpu.VMEM((2, heads, Q, Q), bf16),
                ],
            ),
            out_shape=jax.ShapeDtypeStruct((rows, tokens), bf16),
            input_output_aliases={14: 0} if before else {},
            compiler_params=params,
            cost_estimate=pl.CostEstimate(
                flops=2 * tokens_here * (Q * N + rows * Q + bits * rows * N),
                bytes_accessed=4 * tokens_here * (rows + N),
                transcendentals=heads * tokens_here * Q,
            ),
            name="outputs",
        )(ids, core, own_skip, x_heads, *keys, *queries, low, high, cumulative, offset, decay, level_rows, *before)
    return out


def solution(mesh):
    x = mesh.shape["head"] // CORES
    y = math.gcd(mesh.shape["seq"], x)
    z = mesh.shape["seq"] // y
    split_mesh = jax.sharding.Mesh(mesh.devices.reshape(z, y, x, CORES), ("z", "y", "x", "core"))
    seq = ("z", "y")
    head = ("x", "core")
    in_specs = (
        P((*head, *seq), None),
        P((*seq, *head), None),
        P((*seq, *head), None),
        P(head, seq),
        P(head, seq),
        P(head, None, seq),
        P(head),
    )
    out_specs = P((*head, *seq), None)
    return jax.shard_map(
        on_device, mesh=split_mesh, in_specs=in_specs, out_specs=out_specs, check_vma=False
    )
```

profile of v0, /device:TPU:0, one launch (start us, length us, event | category | flops | bytes accessed | tf_op | source)
XLA Modules:
  0.0 200.5 jit_solution(408059902813821666)
XLA Ops:
  0.0 4.0 %collective-permute-start.1 = (bf16[1024,128]{1,0:T(8,128)(2,1)}, bf16[1024,128]{1,0:T(8,128)(2,1)S(1)}, u32[]{:S(2)}, u32[]{:S(2)}) collective-permute-start(bf16[1024,128]{1,0:T(8,128)(2,1)} %param.8), channel_id=1, source_target_pairs={{0,16},{8,24},{16,0},{24,8},{1,17},{9,25},{17,1},{25,9},{2,18},{10... | collective-permute-start | bytes 786440 | tf_op jit(solution)/shard_map/ppermute | solution.py:237
  4.0 1.6 collective-permute-start
  5.6 1.0 copy.13
  6.6 1.0 copy.14
  7.7 0.8 pad_maximum_fusion
  8.5 3.5 %all-to-all-start = ((f32[8,4,16,256]{3,2,1,0:T(8,128)}), f32[8,4,16,256]{3,2,1,0:T(8,128)S(1)}, u32[]{:S(2)}, u32[]{:S(2)}) async-start(f32[8,4,16,256]{3,2,1,0:T(8,128)} %bitcast.3), calls=%async_computation | async-start | bytes 1048576 | tf_op jit(solution)/shard_map/all_to_all | solution.py:296
  12.0 5.0 %collective-permute-done.1 = bf16[1024,128]{1,0:T(8,128)(2,1)S(1)} collective-permute-done((bf16[1024,128]{1,0:T(8,128)(2,1)}, bf16[1024,128]{1,0:T(8,128)(2,1)S(1)}, u32[]{:S(2)}, u32[]{:S(2)}) %collective-permute-start.1) | collective-permute-done | bytes 262176 | tf_op jit(solution)/shard_map/ppermute | solution.py:237
  17.0 0.7 collective-permute-start.2
  17.8 1.7 constant_dynamic-update-slice_fusion.3
  19.4 0.7 constant_dynamic-update-slice_fusion.2
  20.2 0.7 constant_dynamic-update-slice_fusion.1
  20.9 9.6 %collective-permute-done.2 = bf16[1024,128]{1,0:T(8,128)(2,1)S(1)} collective-permute-done((bf16[1024,128]{1,0:T(8,128)(2,1)S(1)}, bf16[1024,128]{1,0:T(8,128)(2,1)S(1)}, u32[]{:S(2)}, u32[]{:S(2)}) %collective-permute-start.2) | collective-permute-done | bytes 262176 | tf_op jit(solution)/shard_map/ppermute | solution.py:237
  31.2 1.5 collective-permute-start.3
  32.8 1.5 collective-permute-start.5
  34.3 1.3 collective-permute-start.9
  35.6 2.4 %collective-permute-start.8 = (bf16[1024,128]{1,0:T(8,128)(2,1)}, bf16[1024,128]{1,0:T(8,128)(2,1)S(1)}, u32[]{:S(2)}, u32[]{:S(2)}) collective-permute-start(bf16[1024,128]{1,0:T(8,128)(2,1)} %param.9), channel_id=1, source_target_pairs={{0,8},{8,0},{16,24},{24,16},{1,9},{9,1},{17,25},{25,17},{2,10},{10... | collective-permute-start | bytes 786440 | tf_op jit(solution)/shard_map/ppermute | solution.py:237
  38.1 10.7 %collective-permute-done.9 = bf16[1024,128]{1,0:T(8,128)(2,1)S(1)} collective-permute-done((bf16[1024,128]{1,0:T(8,128)(2,1)}, bf16[1024,128]{1,0:T(8,128)(2,1)S(1)}, u32[]{:S(2)}, u32[]{:S(2)}) %collective-permute-start.9) | collective-permute-done | bytes 262176 | tf_op jit(solution)/shard_map/ppermute | solution.py:237
  48.8 1.7 constant_dynamic-update-slice_fusion.9
  51.2 0.7 constant_dynamic-update-slice_fusion.7
  51.9 4.4 %collective-permute-done.10 = bf16[1024,128]{1,0:T(8,128)(2,1)S(1)} collective-permute-done((bf16[1024,128]{1,0:T(8,128)(2,1)S(1)}, bf16[1024,128]{1,0:T(8,128)(2,1)S(1)}, u32[]{:S(2)}, u32[]{:S(2)}) %collective-permute-start.10) | collective-permute-done | bytes 262176 | tf_op jit(solution)/shard_map/ppermute | solution.py:237
  58.2 1.5 collective-permute-start.13
  60.2 0.9 slice.17
  61.1 11.4 %collective-permute-done.4 = bf16[2048,128]{1,0:T(8,128)(2,1)S(1)} collective-permute-done((bf16[2048,128]{1,0:T(8,128)(2,1)S(1)}, bf16[2048,128]{1,0:T(8,128)(2,1)S(1)}, u32[]{:S(2)}, u32[]{:S(2)}) %collective-permute-start.4) | collective-permute-done | bytes 524320 | tf_op jit(solution)/shard_map/ppermute | solution.py:237
  72.5 1.5 collective-permute-start.6
  74.0 2.7 %convert_element_type.3 = bf16[16,8,4096]{2,1,0:T(8,128)(2,1)} convert(f32[16,8,4096]{2,1,0:T(8,128)} %param.12) | non-fusion elementwise | flops 524288 | bytes 3145728 | tf_op jit(solution)/shard_map/convert_element_type | solution.py:299
  76.7 4.5 %all-to-all-start.1 = ((bf16[8,16,4096]{2,1,0:T(8,128)(2,1)}), bf16[8,16,4096]{2,1,0:T(8,128)(2,1)S(1)}, u32[]{:S(2)}, u32[]{:S(2)}) async-start(bf16[8,16,4096]{2,1,0:T(8,128)(2,1)} %bitcast.30), calls=%async_computation.1 | async-start | bytes 2097152 | tf_op jit(solution)/shard_map/all_to_all | solution.py:298
  81.2 1.9 constant_dynamic-update-slice_fusion.5
  83.4 1.9 slice.18
  85.3 6.7 %collective-permute-done.6 = bf16[2048,128]{1,0:T(8,128)(2,1)} collective-permute-done((bf16[2048,128]{1,0:T(8,128)(2,1)}, bf16[2048,128]{1,0:T(8,128)(2,1)}, u32[]{:S(2)}, u32[]{:S(2)}) %collective-permute-start.6) | collective-permute-done | bytes 524320 | tf_op jit(solution)/shard_map/ppermute | solution.py:237
  92.5 1.9 constant_dynamic-update-slice_fusion.4.mine_ref.my_key_ref
  94.4 9.1 %collective-permute-done.13.my_query_ref = bf16[4096,128]{1,0:T(8,128)(2,1)} collective-permute-done((bf16[4096,128]{1,0:T(8,128)(2,1)}, bf16[4096,128]{1,0:T(8,128)(2,1)}, u32[]{:S(2)}, u32[]{:S(2)}) %collective-permute-start.13) | collective-permute-done | bytes 1048608 | tf_op jit(solution)/shard_map/ppermute | solution.py:237
  103.5 1.9 slice.19
  105.9 1.5 collective-permute-start.14
  107.4 7.2 %collective-permute-done.12 = bf16[2048,128]{1,0:T(8,128)(2,1)} collective-permute-done((bf16[2048,128]{1,0:T(8,128)(2,1)}, bf16[2048,128]{1,0:T(8,128)(2,1)}, u32[]{:S(2)}, u32[]{:S(2)}) %collective-permute-start.12) | collective-permute-done | bytes 524320 | tf_op jit(solution)/shard_map/ppermute | solution.py:237
  114.6 1.9 constant_dynamic-update-slice_fusion.11
  116.5 3.6 %collective-permute-done.14 = bf16[2048,128]{1,0:T(8,128)(2,1)} collective-permute-done((bf16[2048,128]{1,0:T(8,128)(2,1)}, bf16[2048,128]{1,0:T(8,128)(2,1)}, u32[]{:S(2)}, u32[]{:S(2)}) %collective-permute-start.14) | collective-permute-done | bytes 524320 | tf_op jit(solution)/shard_map/ppermute | solution.py:237
  120.1 1.9 constant_dynamic-update-slice_fusion.10.my_query_ref
  123.8 5.3 %gates.1 = (f32[2,128,256]{2,1,0:T(8,128)}, f32[2,128,256]{2,1,0:T(8,128)}, f32[2,128,256]{2,1,0:T(8,128)}, f32[2,1024,128]{2,1,0:T(8,128)}, f32[2,1024,128]{2,1,0:T(8,128)}) custom-call(f32[8,4,16,256]{3,2,1,0:T(8,128)} %copy-done.3), custom_call_target="tpu_custom_call" | custom-call | tf_op jit(solution)/shard_map/gates/pallas_call | solution.py:314
  129.1 5.2 %states.5 = (bf16[4,7,128,128]{3,2,1,0:T(8,128)(2,1)}, f32[4,128,128]{2,1,0:T(8,128)}) custom-call(s32[4]{0:T(128)} %copy-done.5, s32[1]{0:T(128)} %bitcast.core_ref, bf16[128,32768]{1,0:T(8,128)(2,1)} %x_ref.15, bf16[4096,128]{1,0:T(8,128)(2,1)} %constant_dynamic-update-slice_fusion.mine_ref.my_key_ref, ...), custom_call_target="tpu_custom_call" | custom-call | flops 268435456 | bytes 8388608 | tf_op jit(solution)/shard_map/states/pallas_call | solution.py:338
  134.4 5.3 %states.6 = (bf16[4,7,128,128]{3,2,1,0:T(8,128)(2,1)}, f32[4,128,128]{2,1,0:T(8,128)}) custom-call(s32[4]{0:T(128)} %copy-done.8, s32[1]{0:T(128)} %bitcast.core_ref, bf16[128,32768]{1,0:T(8,128)(2,1)} %x_ref.15, bf16[4096,128]{1,0:T(8,128)(2,1)} %copy-done.2, bf16[4096,128]{1,0:T(8,128)(2,1)} %collective-permute-done.17.other_ref.other_key_ref, ...), custom_call_target="tpu_custom_call" | custom-call | flops 268435456 | bytes 8388608 | tf_op jit(solution)/shard_map/states/pallas_call | solution.py:338
  139.6 5.2 %states.7 = (bf16[4,7,128,128]{3,2,1,0:T(8,128)(2,1)}, f32[4,128,128]{2,1,0:T(8,128)}) custom-call(s32[4]{0:T(128)} %copy-done.7, s32[1]{0:T(128)} %bitcast.core_ref, bf16[128,32768]{1,0:T(8,128)(2,1)} %x_ref.15, bf16[4096,128]{1,0:T(8,128)(2,1)} %copy-done.1, bf16[4096,128]{1,0:T(8,128)(2,1)} %collective-permute-done.18.other_ref.other_key_ref, ...), custom_call_target="tpu_custom_call" | custom-call | flops 268435456 | bytes 8388608 | tf_op jit(solution)/shard_map/states/pallas_call | solution.py:338
  144.8 5.3 %states.4 = (bf16[4,7,128,128]{3,2,1,0:T(8,128)(2,1)}, f32[4,128,128]{2,1,0:T(8,128)}) custom-call(s32[4]{0:T(128)} %copy-done.6, s32[1]{0:T(128)} %bitcast.core_ref, bf16[128,32768]{1,0:T(8,128)(2,1)} %x_ref.15, bf16[4096,128]{1,0:T(8,128)(2,1)} %constant_dynamic-update-slice_fusion.4.mine_ref.my_key_ref, ...), custom_call_target="tpu_custom_call" | custom-call | flops 268435456 | bytes 8388608 | tf_op jit(solution)/shard_map/states/pallas_call | solution.py:338
  150.1 3.1 %tree.1.high_ref = bf16[16,128,128]{2,1,0:T(8,128)(2,1)} custom-call(s32[16]{0:T(128)} %pad_add_fusion.groups_ref, f32[2,1024,128]{2,1,0:T(8,128)} %get-tuple-element.22.merge_ref, f32[4,128,128]{2,1,0:T(8,128)} %get-tuple-element.24.refs_0_, f32[4,128,128]{2,1,0:T(8,128)} %get-tuple-element.25.refs_1_, f32[4,128,128]{2,1,0:T(8,128)} %get-tuple-element.26.refs_2_, ...), custom_call_target="tpu_custom_call" | custom-call | tf_op jit(solution)/shard_map/tree/pallas_call | solution.py:362
  153.3 1.0 copy-done
  154.2 11.5 %outputs.4.refs_0_ = bf16[128,32768]{1,0:T(8,128)(2,1)} custom-call(s32[4]{0:T(128)} %copy-done.5, s32[1]{0:T(128)} %bitcast.core_ref, f32[2]{0:T(128)} %dynamic_slice.3.skip_ref, bf16[128,32768]{1,0:T(8,128)(2,1)} %x_ref.15, bf16[4096,128]{1,0:T(8,128)(2,1)} %constant_dynamic-update-slice_fusion.mine_ref.my_key_ref, ...), custom_call_target="tpu_custom_call" | custom-call | flops 2952790016 | bytes 8388608 | tf_op jit(solution)/shard_map/outputs/pallas_call | solution.py:380
  165.8 11.5 %outputs.5.refs_0_ = bf16[128,32768]{1,0:T(8,128)(2,1)} custom-call(s32[4]{0:T(128)} %copy-done.8, s32[1]{0:T(128)} %bitcast.core_ref, f32[2]{0:T(128)} %dynamic_slice.3.skip_ref, bf16[128,32768]{1,0:T(8,128)(2,1)} %x_ref.15, bf16[4096,128]{1,0:T(8,128)(2,1)} %copy-done.2, ...), custom_call_target="tpu_custom_call", output_to_operand_aliasing={{}: (14, {})} | custom-call | flops 2952790016 | bytes 8388608 | tf_op jit(solution)/shard_map/outputs/pallas_call | solution.py:380
  177.4 11.6 %outputs.6.refs_0_ = bf16[128,32768]{1,0:T(8,128)(2,1)} custom-call(s32[4]{0:T(128)} %copy-done.7, s32[1]{0:T(128)} %bitcast.core_ref, f32[2]{0:T(128)} %dynamic_slice.3.skip_ref, bf16[128,32768]{1,0:T(8,128)(2,1)} %x_ref.15, bf16[4096,128]{1,0:T(8,128)(2,1)} %copy-done.1, ...), custom_call_target="tpu_custom_call", output_to_operand_aliasing={{}: (14, {})} | custom-call | flops 2952790016 | bytes 8388608 | tf_op jit(solution)/shard_map/outputs/pallas_call | solution.py:380
  188.9 11.5 %outputs.7 = bf16[128,32768]{1,0:T(8,128)(2,1)} custom-call(s32[4]{0:T(128)} %copy-done.6, s32[1]{0:T(128)} %bitcast.core_ref, f32[2]{0:T(128)} %dynamic_slice.3.skip_ref, bf16[128,32768]{1,0:T(8,128)(2,1)} %x_ref.15, bf16[4096,128]{1,0:T(8,128)(2,1)} %constant_dynamic-update-slice_fusion.4.mine_ref.my_key_ref, ...), custom_call_target="tpu_custom_call", output_to_operand_aliasing={{}: (14, {})} | custom-call | flops 2952790016 | bytes 8388608 | tf_op jit(solution)/shard_map/outputs/pallas_call | solution.py:380
  (56 shorter events, 7.1 us)
Async XLA Ops:
  0.0 17.0 %collective-permute-start.1 = (bf16[1024,128]{1,0:T(8,128)(2,1)}, bf16[1024,128]{1,0:T(8,128)(2,1)S(1)}, u32[]{:S(2)}, u32[]{:S(2)}) collective-permute-start(bf16[1024,128]{1,0:T(8,128)(2,1)} %param.8), channel_id=1, source_target_pairs={{0,16},{8,24},{16,0},{24,8},{1,17},{9,25},{17,1},{25,9},{2,18},{10... | collective-permute-start | bytes 786440 | tf_op jit(solution)/shard_map/ppermute | solution.py:237
  4.0 15.4 %collective-permute-start = (bf16[1024,128]{1,0:T(8,128)(2,1)}, bf16[1024,128]{1,0:T(8,128)(2,1)S(1)}, u32[]{:S(2)}, u32[]{:S(2)}) collective-permute-start(bf16[1024,128]{1,0:T(8,128)(2,1)} %param.8), channel_id=1, source_target_pairs={{0,8},{8,0},{16,24},{24,16},{1,9},{9,1},{17,25},{25,17},{2,10},{10... | collective-permute-start | bytes 786440 | tf_op jit(solution)/shard_map/ppermute | solution.py:237
  8.5 25.8 %all-to-all-start = ((f32[8,4,16,256]{3,2,1,0:T(8,128)}), f32[8,4,16,256]{3,2,1,0:T(8,128)S(1)}, u32[]{:S(2)}, u32[]{:S(2)}) async-start(f32[8,4,16,256]{3,2,1,0:T(8,128)} %bitcast.3), calls=%async_computation | async-start | bytes 1048576 | tf_op jit(solution)/shard_map/all_to_all | solution.py:296
  17.0 13.5 %collective-permute-start.2 = (bf16[1024,128]{1,0:T(8,128)(2,1)S(1)}, bf16[1024,128]{1,0:T(8,128)(2,1)S(1)}, u32[]{:S(2)}, u32[]{:S(2)}) collective-permute-start(bf16[1024,128]{1,0:T(8,128)(2,1)S(1)} %collective-permute-done.1), channel_id=1, source_target_pairs={{0,8},{8,0},{16,24},{24,16},{1,9},{9,1},{17,25},{25,17},{2,10},{10... | collective-permute-start | bytes 786440 | tf_op jit(solution)/shard_map/ppermute | solution.py:237
  20.2 102.3 %copy-start.9 = (f32[16]{0:T(128)S(1)}, f32[16]{0:T(128)}, u32[]{:S(2)}) copy-start(f32[16]{0:T(128)} %param.13) | copy-start | bytes 196
  31.2 26.3 %collective-permute-start.3 = (bf16[4096,128]{1,0:T(8,128)(2,1)}, bf16[4096,128]{1,0:T(8,128)(2,1)S(1)}, u32[]{:S(2)}, u32[]{:S(2)}) collective-permute-start(bf16[4096,128]{1,0:T(8,128)(2,1)} %constant_dynamic-update-slice_fusion.mine_ref.my_key_ref), channel_id=1, source_target_pairs={{0,2},{2,0},{1,3},{3,1},{4,6},{6,4},{5,7},{7,5},{8,10},{10,8},{9,1... | collective-permute-start | bytes 3145736 | tf_op jit(solution)/shard_map/ppermute | solution.py:237
  32.8 26.9 %collective-permute-start.5 = (bf16[4096,128]{1,0:T(8,128)(2,1)}, bf16[4096,128]{1,0:T(8,128)(2,1)S(1)}, u32[]{:S(2)}, u32[]{:S(2)}) collective-permute-start(bf16[4096,128]{1,0:T(8,128)(2,1)} %constant_dynamic-update-slice_fusion.mine_ref.my_key_ref), channel_id=1, source_target_pairs={{0,4},{4,0},{1,5},{5,1},{2,6},{6,2},{3,7},{7,3},{8,12},{12,8},{9,1... | collective-permute-start | bytes 3145736 | tf_op jit(solution)/shard_map/ppermute | solution.py:237
  34.3 42.4 %copy-start.3 = (f32[8,4,16,256]{3,2,1,0:T(8,128)}, f32[8,4,16,256]{3,2,1,0:T(8,128)S(1)}, u32[]{:S(2)}) copy-start(f32[8,4,16,256]{3,2,1,0:T(8,128)S(1)} %all-to-all-done.gates_ref) | copy-start | bytes 1572868
  34.3 14.5 %collective-permute-start.9 = (bf16[1024,128]{1,0:T(8,128)(2,1)}, bf16[1024,128]{1,0:T(8,128)(2,1)S(1)}, u32[]{:S(2)}, u32[]{:S(2)}) collective-permute-start(bf16[1024,128]{1,0:T(8,128)(2,1)} %param.9), channel_id=1, source_target_pairs={{0,16},{8,24},{16,0},{24,8},{1,17},{9,25},{17,1},{25,9},{2,18},{10... | collective-permute-start | bytes 786440 | tf_op jit(solution)/shard_map/ppermute | solution.py:237
  35.6 14.8 %collective-permute-start.8 = (bf16[1024,128]{1,0:T(8,128)(2,1)}, bf16[1024,128]{1,0:T(8,128)(2,1)S(1)}, u32[]{:S(2)}, u32[]{:S(2)}) collective-permute-start(bf16[1024,128]{1,0:T(8,128)(2,1)} %param.9), channel_id=1, source_target_pairs={{0,8},{8,0},{16,24},{24,16},{1,9},{9,1},{17,25},{25,17},{2,10},{10... | collective-permute-start | bytes 786440 | tf_op jit(solution)/shard_map/ppermute | solution.py:237
  48.8 7.5 %collective-permute-start.10 = (bf16[1024,128]{1,0:T(8,128)(2,1)S(1)}, bf16[1024,128]{1,0:T(8,128)(2,1)S(1)}, u32[]{:S(2)}, u32[]{:S(2)}) collective-permute-start(bf16[1024,128]{1,0:T(8,128)(2,1)S(1)} %collective-permute-done.9), channel_id=1, source_target_pairs={{0,8},{8,0},{16,24},{24,16},{1,9},{9,1},{17,25},{25,17},{2,10},{10... | collective-permute-start | bytes 786440 | tf_op jit(solution)/shard_map/ppermute | solution.py:237
  57.0 26.4 %collective-permute-start.11 = (bf16[4096,128]{1,0:T(8,128)(2,1)}, bf16[4096,128]{1,0:T(8,128)(2,1)}, u32[]{:S(2)}, u32[]{:S(2)}) collective-permute-start(bf16[4096,128]{1,0:T(8,128)(2,1)} %constant_dynamic-update-slice_fusion.6.my_query_ref), channel_id=1, source_target_pairs={{0,2},{2,0},{1,3},{3,1},{4,6},{6,4},{5,7},{7,5},{8,10},{10,8},{9,1... | collective-permute-start | bytes 3145736 | tf_op jit(solution)/shard_map/ppermute | solution.py:237
  57.5 76.8 %copy-start.2 = (bf16[4096,128]{1,0:T(8,128)(2,1)}, bf16[4096,128]{1,0:T(8,128)(2,1)S(1)}, u32[]{:S(2)}) copy-start(bf16[4096,128]{1,0:T(8,128)(2,1)S(1)} %collective-permute-done.3.mine_ref.my_key_ref) | copy-start | bytes 3145732
  57.6 14.9 %collective-permute-start.4 = (bf16[2048,128]{1,0:T(8,128)(2,1)S(1)}, bf16[2048,128]{1,0:T(8,128)(2,1)S(1)}, u32[]{:S(2)}, u32[]{:S(2)}) collective-permute-start(bf16[2048,128]{1,0:T(8,128)(2,1)S(1)} %slice.16), channel_id=1, source_target_pairs={{0,4},{4,0},{1,5},{5,1},{2,6},{6,2},{3,7},{7,3},{8,12},{12,8},{9,1... | collective-permute-start | bytes 1572872 | tf_op jit(solution)/shard_map/ppermute | solution.py:237
  58.2 45.3 %collective-permute-start.13 = (bf16[4096,128]{1,0:T(8,128)(2,1)}, bf16[4096,128]{1,0:T(8,128)(2,1)}, u32[]{:S(2)}, u32[]{:S(2)}) collective-permute-start(bf16[4096,128]{1,0:T(8,128)(2,1)} %constant_dynamic-update-slice_fusion.6.my_query_ref), channel_id=1, source_target_pairs={{0,4},{4,0},{1,5},{5,1},{2,6},{6,2},{3,7},{7,3},{8,12},{12,8},{9,1... | collective-permute-start | bytes 3145736 | tf_op jit(solution)/shard_map/ppermute | solution.py:237
  59.7 45.7 %collective-permute-start.16 = (bf16[4096,128]{1,0:T(8,128)(2,1)}, bf16[4096,128]{1,0:T(8,128)(2,1)}, u32[]{:S(2)}, u32[]{:S(2)}) collective-permute-start(bf16[4096,128]{1,0:T(8,128)(2,1)} %constant_dynamic-update-slice_fusion.mine_ref.my_key_ref), channel_id=1, source_target_pairs={{0,1},{1,0},{2,3},{3,2},{4,5},{5,4},{6,7},{7,6},{8,9},{9,8},{10,11... | collective-permute-start | bytes 3145736 | tf_op jit(solution)/shard_map/ppermute | solution.py:237
  59.7 74.7 %copy-start.1 = (bf16[4096,128]{1,0:T(8,128)(2,1)}, bf16[4096,128]{1,0:T(8,128)(2,1)S(1)}, u32[]{:S(2)}) copy-start(bf16[4096,128]{1,0:T(8,128)(2,1)S(1)} %collective-permute-done.5.mine_ref.my_key_ref) | copy-start | bytes 3145732
  59.7 46.2 %collective-permute-start.17 = (bf16[4096,128]{1,0:T(8,128)(2,1)S(1)}, bf16[4096,128]{1,0:T(8,128)(2,1)}, u32[]{:S(2)}, u32[]{:S(2)}) collective-permute-start(bf16[4096,128]{1,0:T(8,128)(2,1)S(1)} %collective-permute-done.3.mine_ref.my_key_ref), channel_id=1, source_target_pairs={{0,1},{1,0},{2,3},{3,2},{4,5},{5,4},{6,7},{7,6},{8,9},{9,8},{10,11... | collective-permute-start | bytes 3145736 | tf_op jit(solution)/shard_map/ppermute | solution.py:237
  72.5 4.2 %copy-start.4 = (bf16[2048,128]{1,0:T(8,128)(2,1)}, bf16[2048,128]{1,0:T(8,128)(2,1)S(1)}, u32[]{:S(2)}) copy-start(bf16[2048,128]{1,0:T(8,128)(2,1)S(1)} %collective-permute-done.4) | copy-start | bytes 1572868
  72.5 19.5 %collective-permute-start.6 = (bf16[2048,128]{1,0:T(8,128)(2,1)}, bf16[2048,128]{1,0:T(8,128)(2,1)}, u32[]{:S(2)}, u32[]{:S(2)}) collective-permute-start(bf16[2048,128]{1,0:T(8,128)(2,1)} %slice.17), channel_id=1, source_target_pairs={{0,2},{2,0},{1,3},{3,1},{4,6},{6,4},{5,7},{7,5},{8,10},{10,8},{9,1... | collective-permute-start | bytes 1572872 | tf_op jit(solution)/shard_map/ppermute | solution.py:237
  76.7 76.5 %all-to-all-start.1 = ((bf16[8,16,4096]{2,1,0:T(8,128)(2,1)}), bf16[8,16,4096]{2,1,0:T(8,128)(2,1)S(1)}, u32[]{:S(2)}, u32[]{:S(2)}) async-start(bf16[8,16,4096]{2,1,0:T(8,128)(2,1)} %bitcast.30), calls=%async_computation.1 | async-start | bytes 2097152 | tf_op jit(solution)/shard_map/all_to_all | solution.py:298
  83.4 38.6 %collective-permute-start.18 = (bf16[4096,128]{1,0:T(8,128)(2,1)S(1)}, bf16[4096,128]{1,0:T(8,128)(2,1)}, u32[]{:S(2)}, u32[]{:S(2)}) collective-permute-start(bf16[4096,128]{1,0:T(8,128)(2,1)S(1)} %collective-permute-done.5.mine_ref.my_key_ref), channel_id=1, source_target_pairs={{0,1},{1,0},{2,3},{3,2},{4,5},{5,4},{6,7},{7,6},{8,9},{9,8},{10,11... | collective-permute-start | bytes 3145736 | tf_op jit(solution)/shard_map/ppermute | solution.py:237
  92.0 22.6 %collective-permute-start.12 = (bf16[2048,128]{1,0:T(8,128)(2,1)}, bf16[2048,128]{1,0:T(8,128)(2,1)}, u32[]{:S(2)}, u32[]{:S(2)}) collective-permute-start(bf16[2048,128]{1,0:T(8,128)(2,1)} %slice.18), channel_id=1, source_target_pairs={{0,4},{4,0},{1,5},{5,1},{2,6},{6,2},{3,7},{7,3},{8,12},{12,8},{9,1... | collective-permute-start | bytes 1572872 | tf_op jit(solution)/shard_map/ppermute | solution.py:237
  103.5 49.8 %collective-permute-start.21 = (bf16[4096,128]{1,0:T(8,128)(2,1)}, bf16[4096,128]{1,0:T(8,128)(2,1)}, u32[]{:S(2)}, u32[]{:S(2)}) collective-permute-start(bf16[4096,128]{1,0:T(8,128)(2,1)} %constant_dynamic-update-slice_fusion.6.my_query_ref), channel_id=1, source_target_pairs={{0,1},{1,0},{2,3},{3,2},{4,5},{5,4},{6,7},{7,6},{8,9},{9,8},{10,11... | collective-permute-start | bytes 3145736 | tf_op jit(solution)/shard_map/ppermute | solution.py:237
  105.4 39.5 %collective-permute-start.7 = (bf16[4096,128]{1,0:T(8,128)(2,1)}, bf16[4096,128]{1,0:T(8,128)(2,1)}, u32[]{:S(2)}, u32[]{:S(2)}) collective-permute-start(bf16[4096,128]{1,0:T(8,128)(2,1)} %constant_dynamic-update-slice_fusion.4.mine_ref.my_key_ref), channel_id=1, source_target_pairs={{0,1},{1,0},{2,3},{3,2},{4,5},{5,4},{6,7},{7,6},{8,9},{9,8},{10,11... | collective-permute-start | bytes 3145736 | tf_op jit(solution)/shard_map/ppermute | solution.py:237
  105.9 14.2 %collective-permute-start.14 = (bf16[2048,128]{1,0:T(8,128)(2,1)}, bf16[2048,128]{1,0:T(8,128)(2,1)}, u32[]{:S(2)}, u32[]{:S(2)}) collective-permute-start(bf16[2048,128]{1,0:T(8,128)(2,1)} %slice.19), channel_id=1, source_target_pairs={{0,2},{2,0},{1,3},{3,1},{4,6},{6,4},{5,7},{7,5},{8,10},{10,8},{9,1... | collective-permute-start | bytes 1572872 | tf_op jit(solution)/shard_map/ppermute | solution.py:237
  107.4 32.2 %copy-start.7 = (s32[4]{0:T(128)}, s32[4]{0:T(128)S(1)}, u32[]{:S(2)}) copy-start(s32[4]{0:T(128)S(1)} %broadcast_add_fusion.groups_ref) | copy-start | bytes 52
  107.4 32.2 %copy-start.6 = (s32[4]{0:T(128)}, s32[4]{0:T(128)S(1)}, u32[]{:S(2)}) copy-start(s32[4]{0:T(128)S(1)} %broadcast_add_fusion.3.groups_ref) | copy-start | bytes 52
  107.4 26.9 %copy-start.8 = (s32[4]{0:T(128)}, s32[4]{0:T(128)S(1)}, u32[]{:S(2)}) copy-start(s32[4]{0:T(128)S(1)} %broadcast_add_fusion.2.groups_ref) | copy-start | bytes 52
  114.6 51.2 %collective-permute-start.20 = (bf16[4096,128]{1,0:T(8,128)(2,1)}, bf16[4096,128]{1,0:T(8,128)(2,1)}, u32[]{:S(2)}, u32[]{:S(2)}) collective-permute-start(bf16[4096,128]{1,0:T(8,128)(2,1)} %collective-permute-done.11.my_query_ref), channel_id=1, source_target_pairs={{0,1},{1,0},{2,3},{3,2},{4,5},{5,4},{6,7},{7,6},{8,9},{9,8},{10,11... | collective-permute-start | bytes 3145736 | tf_op jit(solution)/shard_map/ppermute | solution.py:237
  120.1 57.3 %collective-permute-start.19 = (bf16[4096,128]{1,0:T(8,128)(2,1)}, bf16[4096,128]{1,0:T(8,128)(2,1)}, u32[]{:S(2)}, u32[]{:S(2)}) collective-permute-start(bf16[4096,128]{1,0:T(8,128)(2,1)} %collective-permute-done.13.my_query_ref), channel_id=1, source_target_pairs={{0,1},{1,0},{2,3},{3,2},{4,5},{5,4},{6,7},{7,6},{8,9},{9,8},{10,11... | collective-permute-start | bytes 3145736 | tf_op jit(solution)/shard_map/ppermute | solution.py:237
  122.0 66.9 %collective-permute-start.15 = (bf16[4096,128]{1,0:T(8,128)(2,1)}, bf16[4096,128]{1,0:T(8,128)(2,1)}, u32[]{:S(2)}, u32[]{:S(2)}) collective-permute-start(bf16[4096,128]{1,0:T(8,128)(2,1)} %constant_dynamic-update-slice_fusion.10.my_query_ref), channel_id=1, source_target_pairs={{0,1},{1,0},{2,3},{3,2},{4,5},{5,4},{6,7},{7,6},{8,9},{9,8},{10,11... | collective-permute-start | bytes 3145736 | tf_op jit(solution)/shard_map/ppermute | solution.py:237
  122.5 6.6 %copy-start.5 = (s32[4]{0:T(128)}, s32[4]{0:T(128)S(1)}, u32[]{:S(2)}) copy-start(s32[4]{0:T(128)S(1)} %broadcast_add_fusion.1.groups_ref) | copy-start | bytes 52
  153.3 1.0 copy-start
where the time goes:
time: 202 us; the launch traced here: 200 us
  Pallas kernels  75.6 us (37%)
  waiting for transfers between devices  68.2 us (34%)
  starting transfers between devices  28.8 us (14%)
  local copies, waits for them, and re-layouts  23.6 us (12%)
  other arithmetic  4.23 us (2%)
    ppermute x22, waiting for transfers between devices, exchange(): return lax.ppermute(value, axis, pairs)  68.2 us
    pallas_call x4, Pallas kernels, on_device(): pl.pallas_call(functools.partial(outputs_kernel, heads, width, group, bit...  46.2 us
    pallas_call x4, Pallas kernels, on_device(): pl.pallas_call(functools.partial(states_kernel, heads, width, group, padd...  21 us
    ppermute x22, starting transfers between devices, exchange(): return lax.ppermute(value, axis, pairs)  20.8 us
    unnamed x30, local copies, waits for them, and re-layouts  13.1 us
    pallas_call x1, Pallas kernels, on_device(): pl.pallas_call(functools.partial(gates_kernel, heads, levels, padded), ou...  5.26 us
    all_to_all x1, starting transfers between devices, on_device(): lax.all_to_all(to_owners(after(level_weight, gates).astype(bf16)), ('z',...  4.46 us
  transfers between devices with their start and end apart: 24, of which 10 were waited for; matrix products, arithmetic and copies ran while one was open for 13% of the time, Pallas kernels for 32%

commit v1 on v0

--- a/solution.py
+++ b/solution.py
@@ -32,8 +32,8 @@
     return high, middle, low
 
 
-def gates_kernel(heads, levels, padded, gates_ref, weight_ref, cum_ref, offset_ref, decay_ref, merge_ref,
-                 log_scratch):
+def gates_kernel(heads, levels, padded, gates_ref, weight_ref, cum_ref, offset_ref, half_ref, decay_ref,
+                 merge_ref, log_scratch):
     shards, _, span_rows, _ = gates_ref.shape
     spans = shards * span_rows
     upper = (
@@ -50,7 +50,10 @@
             span_log = cumulative[:, Q - 1 :]
             cum_ref[head, rows, :] = cumulative
             offset_ref[head, rows, :] = cumulative - jnp.log(step)
-            weight_ref[head, rows, :] = jnp.exp(span_log - cumulative) * step
+            half_log = cumulative[:, HALF - 1 : HALF]
+            weight_ref[head, rows, :HALF] = jnp.exp(half_log - cumulative[:, :HALF]) * step[:, :HALF]
+            weight_ref[head, rows, HALF:] = jnp.exp(span_log - cumulative[:, HALF:]) * step[:, HALF:]
+            half_ref[head, rows, :] = jnp.broadcast_to(jnp.exp(span_log - half_log), (span_rows, N))
             log_scratch[rows, :] = jnp.broadcast_to(span_log, (span_rows, N))
         high, middle, low = exact_parts(log_scratch[...])
 
@@ -84,35 +87,33 @@
     return jnp.where(core == local // half, mine_ref[rows, :], other_ref[rows, :])
 
 
+def scaled(value, rows, width):
+    parts = [value[head * width : (head + 1) * width] * row for head, row in enumerate(rows)]
+    return jnp.concatenate(parts, axis=0) if len(parts) > 1 else parts[0]
+
+
 def merge_blocks(left, right, merge_ref, row, width):
-    parts = []
-    for head in range(merge_ref.shape[0]):
-        rows = slice(head * width, (head + 1) * width)
-        parts.append(left[rows] * merge_ref[head, row : row + 1, :] + right[rows])
-    return jnp.concatenate(parts, axis=0) if len(parts) > 1 else parts[0]
+    return scaled(left, [merge_ref[head, row : row + 1, :] for head in range(merge_ref.shape[0])], width) + right
 
 
 def states_kernel(heads, width, group, padded, groups_ref, core_ref, x_ref, mine_ref, other_ref, weight_ref,
-                  merge_ref, low_ref, total_ref):
+                  half_ref, merge_ref, low_ref, total_ref):
     kept = {}
     for local in range(group):
         columns = slice(local * Q, (local + 1) * Q)
-        parts = [
-            (
-                x_ref[head * width : (head + 1) * width, columns].astype(f32)
-                * weight_ref[head, local : local + 1, :]
-            ).astype(bf16)
-            for head in range(heads)
-        ]
-        weighted = jnp.concatenate(parts, axis=0) if heads > 1 else parts[0]
-        state = dot(weighted, pick(core_ref[0], mine_ref, other_ref, local, group))
+        weights = [weight_ref[head, local : local + 1, :] for head in range(heads)]
+        weighted = scaled(x_ref[:, columns].astype(f32), weights, width).astype(bf16)
+        keys = pick(core_ref[0], mine_ref, other_ref, local, group)
+        first = dot(weighted[:, :HALF], keys[:HALF])
+        low_ref[group + local] = first.astype(bf16)
+        halves = [half_ref[head, local : local + 1, :] for head in range(heads)]
+        state = scaled(first, halves, width) + dot(weighted[:, HALF:], keys[HALF:])
         bit = 0
         while local >> bit & 1:
             state = merge_blocks(kept[bit], state, merge_ref, local * padded + bit + 1, width)
             bit += 1
         kept[bit] = state
-        if local < group - 1:
-            low_ref[local] = state.astype(bf16)
+        low_ref[local] = state.astype(bf16)
     total_ref[...] = state
 
 
@@ -140,7 +141,7 @@
 def outputs_kernel(heads, width, group, bits, padded, groups_ref, core_ref, skip_ref, x_ref, my_key_ref,
                    other_key_ref, my_query_ref, other_query_ref, low_ref, high_ref, cum_ref, offset_ref, decay_ref,
                    level_ref, *refs):
-    out_ref, query_ref, score_ref, mixing_ref = refs[-4:]
+    out_ref, query_ref, score_ref, side_ref = refs[-4:]
     step = groups_ref[pl.program_id(0)]
     low_bits = group.bit_length() - 1
     levels = bits + 1
@@ -155,81 +156,64 @@
 
     @pl.when(pl.program_id(0) == 0)
     def _():
-        mixing_ref[:, :, HALF:, :HALF] = jnp.zeros((2, heads, HALF, HALF), bf16)
-
-    def span_columns(local):
-        return slice(local * Q, (local + 1) * Q)
+        side_ref[:, :, :HALF, HALF:] = jnp.zeros((2, heads, HALF, HALF), bf16)
+        side_ref[:, :, HALF:Q, :HALF] = jnp.zeros((2, heads, HALF, HALF), bf16)
+        side_ref[:, :, Q : Q + N, :HALF] = jnp.zeros((2, heads, N, HALF), bf16)
+
+    def active(local):
+        return [bit for bit in range(bits) if bit >= low_bits or local >> bit & 1]
 
     def score(local):
         slot = local % 2
         query_ref[slot] = jnp.transpose(pick(core_ref[0], my_query_ref, other_query_ref, local, group))
         keys = pick(core_ref[0], my_key_ref, other_key_ref, local, group)
-        upper = dot(keys[:HALF], query_ref[slot])
-        score_ref[slot, :HALF, :HALF] = jnp.where(causal, upper[:, :HALF], 0.0)
-        score_ref[slot, :HALF, HALF:] = upper[:, HALF:]
-        lower = dot(keys[HALF:], query_ref[slot, :, HALF:])
-        score_ref[slot, HALF:, HALF:] = jnp.where(causal, lower, 0.0)
-
-    def mix(local):
+        for half in (slice(0, HALF), slice(HALF, Q)):
+            score_ref[slot, half] = jnp.where(causal, dot(keys[half], query_ref[slot, :, half]), 0.0)
+
+    def prepare(local):
         slot = local % 2
+        columns = slice(local * Q, (local + 1) * Q)
+        weights = level_ref[0, :, columns].astype(f32)
         for head in range(heads):
-            left = cum_ref[head, local : local + 1, :HALF]
-            right = cum_ref[head, local : local + 1, HALF:]
+            cumulative = cum_ref[head, local : local + 1, :]
+            weight = weights[head * levels : (head + 1) * levels]
+            own = cumulative + jnp.log(weight[:1])
             column = offsets[head][:, local : local + 1]
-            upper = jnp.broadcast_to(column[:HALF], (HALF, HALF))
-            lower = jnp.broadcast_to(column[HALF:], (HALF, HALF))
-            mixing_ref[slot, head, :HALF, :HALF] = (
-                score_ref[slot, :HALF, :HALF] * jnp.exp(jnp.minimum(left - upper, 64.0))
-            ).astype(bf16)
-            mixing_ref[slot, head, :HALF, HALF:] = (
-                score_ref[slot, :HALF, HALF:] * jnp.exp(right - upper)
-            ).astype(bf16)
-            mixing_ref[slot, head, HALF:, HALF:] = (
-                score_ref[slot, HALF:, HALF:] * jnp.exp(jnp.minimum(right - lower, 64.0))
-            ).astype(bf16)
-
-    def level_parts(local):
-        slot = local % 2
-        columns = span_columns(local)
-        weights = level_ref[0, :, columns].astype(f32)
-        factors = []
-        for head in range(heads):
+            for half in (slice(0, HALF), slice(HALF, Q)):
+                gaps = jnp.minimum(own[:, half] - column[half], 64.0)
+                side_ref[slot, head, half, half] = (score_ref[slot, half] * jnp.exp(gaps)).astype(bf16)
+            across = jnp.exp(own[:, HALF:] - cumulative[:, HALF - 1 : HALF]).astype(bf16)
+            side_ref[slot, head, Q : Q + N, HALF:] = query_ref[slot, :, HALF:] * across
             decay = decay_ref[head, local * padded : local * padded + levels, :]
             decay = jnp.concatenate([decay] * (Q // N), axis=1)
-            growth = jnp.exp(cum_ref[head, local : local + 1, :] + decay)
-            factors.append(weights[head * levels : (head + 1) * levels] * growth)
-        sums = [None] * heads
-        for bit in range(bits):
+            factors = weight * jnp.exp(cumulative + decay)
+            for place, bit in enumerate(active(local)):
+                rows = slice(Q + (place + 1) * N, Q + (place + 2) * N)
+                side_ref[slot, head, rows, :] = query_ref[slot] * factors[bit + 1 : bit + 2].astype(bf16)
+
+    def finish(local):
+        slot = local % 2
+        columns = slice(local * Q, (local + 1) * Q)
+        states = [low_ref[group + local]]
+        for bit in active(local):
             if bit < low_bits:
-                if not local >> bit & 1:
-                    continue
-                state = low_ref[((local >> bit) << bit) - 1]
+                states.append(low_ref[((local >> bit) << bit) - 1])
             else:
-                state = high_ref[high_slots[bit - low_bits]]
-            part = dot(state, query_ref[slot])
-            for head in range(heads):
-                term = part[head_rows[head]] * factors[head][bit + 1 : bit + 2]
-                sums[head] = term if sums[head] is None else sums[head] + term
-        return sums, [weights[head * levels : head * levels + 1] for head in range(heads)]
-
-    def finish(local, parts):
-        slot = local % 2
-        columns = span_columns(local)
-        sums, own = parts
+                states.append(high_ref[high_slots[bit - low_bits]])
         for head in range(heads):
             values = x_ref[head_rows[head], columns]
-            result = dot(values, mixing_ref[slot, head]) * own[head] + skip_ref[head] * values.astype(f32)
-            if sums[head] is not None:
-                result += sums[head]
-            out_ref[head_rows[head], columns] = result.astype(bf16)
+            left = jnp.concatenate([values] + [state[head_rows[head]] for state in states], axis=1)
+            result = dot(left, side_ref[slot, head, : Q + len(states) * N, :])
+            out_ref[head_rows[head], columns] = (result + skip_ref[head] * values.astype(f32)).astype(bf16)
 
     score(0)
     for local in range(group):
-        parts = level_parts(local)
         if local + 1 < group:
             score(local + 1)
-        mix(local)
-        finish(local, parts)
+        prepare(local)
+        if local:
+            finish(local - 1)
+    finish(group - 1)
 
 
 def exchange(value, axis, distance):
@@ -242,26 +226,41 @@
     for distance in range(1, lax.axis_size("z")):
         low = distance & -distance
         pieces.append(exchange(pieces[distance ^ low], "z", low))
-    return jnp.concatenate(pieces, axis=0)
-
-
-def in_plane(piece):
-    half = piece.shape[0] // 2
+    return pieces[1:]
+
+
+def places():
+    both = [(y, x) for y in range(lax.axis_size("y")) for x in range(lax.axis_size("x"))]
+    return sorted(both, key=lambda place: ((place[0] > 0) + (place[1] > 0), place))
+
+
+def straight(piece):
+    near = {(0, 0): piece}
+    for y, x in places():
+        if (y > 0) != (x > 0):
+            near[y, x] = exchange(piece, "x", x) if x else exchange(piece, "y", y)
+    return near
+
+
+def diagonal(near, by_x, by_y):
     far = {}
-    for distance in range(1, lax.axis_size("x")):
-        far[0, distance] = exchange(piece, "x", distance)
-    for distance in range(1, lax.axis_size("y")):
-        far[distance, 0] = exchange(piece, "y", distance)
-    for y in range(1, lax.axis_size("y")):
-        for x in range(1, lax.axis_size("x")):
-            first = exchange(far[0, x][:half], "y", y)
-            second = exchange(far[y, 0][half:], "x", x)
-            far[y, x] = jnp.concatenate([first, second], axis=0)
-    return {(0, 0): piece, **far}
-
-
-def both_cores(plane):
-    return {place: (piece, exchange(piece, "core", 1)) for place, piece in plane.items()}
+    for y, x in places():
+        if y and x:
+            parts = []
+            if by_x is not None:
+                parts.append(exchange(near[0, x][by_x], "y", y))
+            if by_y is not None:
+                parts.append(exchange(near[y, 0][by_y], "x", x))
+            far[y, x] = parts
+    return far
+
+
+def join(parts):
+    return jnp.concatenate(parts, axis=0) if len(parts) > 1 else parts[0]
+
+
+def with_core(piece):
+    return piece, exchange(piece, "core", 1)
 
 
 def after(value, *others):
@@ -294,53 +293,59 @@
         [log_gate.reshape(head_count, span_rows, Q), step_size.reshape(head_count, span_rows, Q)], axis=1
     )
     gates = lax.all_to_all(to_owners(gates), ("z", "y"), split_axis=0, concat_axis=0, tiled=True)
+    everything = slice(None)
+    key_near = straight(b_proj)
     key_line = along_z(b_proj)
+    query_near = straight(c_proj)
+    query_line = along_z(c_proj)
+    key_near.update({place: join(parts) for place, parts in diagonal(key_near, everything, None).items()})
+    query_near.update({place: join(parts) for place, parts in diagonal(query_near, None, everything).items()})
     level_rows = lax.all_to_all(
         to_owners(after(level_weight, gates).astype(bf16)), ("z", "y"), split_axis=0, concat_axis=0, tiled=True
     )
-    key_sets = both_cores(in_plane(key_line))
-    query_sets = both_cores(in_plane(along_z(after(c_proj, key_line, gates))))
+    keys_here = with_core(jnp.concatenate([key_near[place] for place in places()], axis=0))
+    queries_here = with_core(jnp.concatenate([query_near[place] for place in places()], axis=0))
     first_head = lax.axis_index(("z", "y")) * rows // P_SIZE
     own_skip = lax.dynamic_slice_in_dim(skip, first_head, heads, 0)
     core = lax.axis_index("core").astype(jnp.int32).reshape(1)
 
-    def group_ids(place):
-        z = lax.axis_index("z") ^ jnp.arange(lax.axis_size("z"))
+    def group_ids(place, z=None):
+        z = lax.axis_index("z") ^ jnp.arange(1, lax.axis_size("z")) if z is None else z
         y = lax.axis_index("y") ^ place[0]
         x = lax.axis_index("x") ^ place[1]
         return ((z * lax.axis_size("y") + y) * lax.axis_size("x") + x).astype(jnp.int32)
 
     params = pltpu.CompilerParams(vmem_limit_bytes=VMEM_LIMIT)
-    weight, cumulative, offset, decay, merge = pl.pallas_call(
+    weight, cumulative, offset, half, decay, merge = pl.pallas_call(
         functools.partial(gates_kernel, heads, levels, padded),
         out_shape=[jax.ShapeDtypeStruct((heads, spans, Q), f32)] * 3
+        + [jax.ShapeDtypeStruct((heads, spans, N), f32)]
         + [jax.ShapeDtypeStruct((heads, spans * padded, N), f32)] * 2,
         scratch_shapes=[pltpu.VMEM((spans, N), f32)],
         compiler_params=params,
         name="gates",
     )(gates)
     weight, cumulative, offset = [v.reshape(heads, steps, group, Q) for v in (weight, cumulative, offset)]
+    half = half.reshape(heads, steps, group, N)
 
     x_spec = pl.BlockSpec((rows, group * Q), lambda i, ids, *_: (0, ids[i]))
     token_spec = pl.BlockSpec((block, N), lambda i, *_: (i, 0))
     span_spec = pl.BlockSpec((heads, None, group, Q), lambda i, ids, *_: (0, ids[i], 0, 0))
     level_spec = pl.BlockSpec((heads, group * padded, N), lambda i, ids, *_: (0, ids[i], 0))
-    low_slots = max(group - 1, 1)
+    half_spec = pl.BlockSpec((heads, None, group, N), lambda i, ids, *_: (0, ids[i], 0, 0))
+    low_slots = 2 * group
     low_spec = pl.BlockSpec((None, low_slots, rows, N), lambda i, *_: (i, 0, 0, 0))
 
-    sets = [
-        (group_ids(place), key_sets[place], query_sets[place])
-        for place in sorted(key_sets, key=lambda place: ((place[0] > 0) + (place[1] > 0), place))
-    ]
-    lows, totals = [], []
-    for ids, keys, _ in sets:
+    lows, totals, all_ids = [], [], []
+
+    def states(ids, keys):
         count = ids.shape[0]
         low, total = pl.pallas_call(
             functools.partial(states_kernel, heads, width, group, padded),
             grid_spec=pltpu.PrefetchScalarGridSpec(
                 num_scalar_prefetch=2,
                 grid=(count,),
-                in_specs=[x_spec, token_spec, token_spec, span_spec, level_spec],
+                in_specs=[x_spec, token_spec, token_spec, span_spec, half_spec, level_spec],
                 out_specs=[low_spec, pl.BlockSpec((None, rows, N), lambda i, *_: (i, 0, 0))],
             ),
             out_shape=[
@@ -354,9 +359,22 @@
                 transcendentals=0,
             ),
             name="states",
-        )(ids, core, x_heads, *keys, weight, merge)
+        )(ids, core, x_heads, *keys, weight, half, merge)
         lows.append(low)
         totals.append(total)
+        all_ids.append(ids)
+        return total
+
+    here = jnp.concatenate([group_ids(place, lax.axis_index("z").reshape(1)) for place in places()])
+    total = states(here, keys_here)
+    if key_line:
+        halves = slice(0, block * len(key_line) // 2), slice(block * len(key_line) // 2, None)
+        key_far = straight(jnp.concatenate(key_line, axis=0))
+        query_far = straight(after(jnp.concatenate(query_line, axis=0), weight))
+        key_far.update({place: join(parts) for place, parts in diagonal(key_far, *halves).items()})
+        keys_far = {place: with_core(key_far[place]) for place in places()}
+        for place in places():
+            states(group_ids(place), keys_far[place])
 
     vmem = pl.BlockSpec(memory_space=pltpu.VMEM)
     high = pl.pallas_call(
@@ -370,14 +388,13 @@
         out_shape=jax.ShapeDtypeStruct((steps, rows, N), bf16),
         compiler_params=params,
         name="tree",
-    )(jnp.concatenate([ids for ids, _, _ in sets]), merge, *totals)
-
-    out = None
-    for (ids, keys, queries), low in zip(sets, lows):
+    )(jnp.concatenate(all_ids), merge, *totals)
+
+    def outputs(ids, keys, queries, low, out):
         count = ids.shape[0]
         tokens_here = count * group * Q
         before = [] if out is None else [out]
-        out = pl.pallas_call(
+        return pl.pallas_call(
             functools.partial(outputs_kernel, heads, width, group, bits, padded),
             grid_spec=pltpu.PrefetchScalarGridSpec(
                 num_scalar_prefetch=2,
@@ -403,8 +420,8 @@
                 out_specs=x_spec,
                 scratch_shapes=[
                     pltpu.VMEM((2, N, Q), bf16),
-                    pltpu.VMEM((2, Q, Q), f32),
-                    pltpu.VMEM((2, heads, Q, Q), bf16),
+                    pltpu.VMEM((2, Q, HALF), f32),
+                    pltpu.VMEM((2, heads, Q + levels * N, Q), bf16),
                 ],
             ),
             out_shape=jax.ShapeDtypeStruct((rows, tokens), bf16),
@@ -417,6 +434,17 @@
             ),
             name="outputs",
         )(ids, core, own_skip, x_heads, *keys, *queries, low, high, cumulative, offset, decay, level_rows, *before)
+    out = outputs(here, keys_here, queries_here, lows[0], None)
+    if key_line:
+        query_far = {place: after(piece, out) if any(place) else piece for place, piece in query_far.items()}
+        corners = diagonal(query_far, *halves)
+        queries_far = {place: with_core(piece) for place, piece in query_far.items()}
+        for at, place in enumerate(places()):
+            if at + 2 == len(query_far):
+                for corner, parts in corners.items():
+                    queries_far[corner] = with_core(join([after(part, out) for part in parts]))
+                out = after(out, *[queries_far[corner][0] for corner in corners])
+            out = outputs(group_ids(place), keys_far[place], queries_far[place], lows[1 + at], out)
     return out
 
 

time: 202 us -> 208 us (1.030)
  waiting for transfers between devices: 68.2 us -> 45 us
  Pallas kernels: 75.6 us -> 94 us
  starting transfers between devices: 28.8 us -> 39.2 us
  other arithmetic: 4.23 us -> 6.38 us
    ppermute x22 -> x30, waiting for transfers between devices: 68.2 us -> 45 us  [exchange(): return lax.ppermute(value, axis, pairs)]
    pallas_call x8 -> x10, Pallas kernels: 67.2 us -> 85.6 us  [the longest x5 59.8 us: outputs(): pl.pallas_call(functools.partial(outputs_kernel, heads, width, group, bit...]
    ppermute x22 -> x30, starting transfers between devices: 20.8 us -> 30 us  [exchange(): return lax.ppermute(value, axis, pairs)]
    all_to_all x1, starting transfers between devices: 3.49 us -> 5.64 us  [on_device(): lax.all_to_all(to_owners(gates), ('z', 'y'), split_axis=0, concat_axis=0,...]
    concatenate x4 -> x6, local copies, waits for them, and re-layouts: 5.19 us -> 4.13 us  [the longest x1 1.15 us: on_device(): jnp.concatenate([key_near[place] for place in places()], axis=0)]
    unnamed x30 -> x46, local copies, waits for them, and re-layouts: 13.1 us -> 14.1 us
  transfers between devices with their start and end apart: 24 -> 32, of which waited for: 10 -> 6; matrix products, arithmetic and copies ran while one was open for 13% -> 11% of each run, Pallas kernels for 32% -> 40%
where the time goes in v1:
time: 208 us; the launch traced here: 207 us
  Pallas kernels  94 us (45%)
  waiting for transfers between devices  45 us (22%)
  starting transfers between devices  39.2 us (19%)
  local copies, waits for them, and re-layouts  21.7 us (10%)
  other arithmetic  6.38 us (3%)
    pallas_call x5, Pallas kernels, outputs(): pl.pallas_call(functools.partial(outputs_kernel, heads, width, group, bit...  59.8 us
    ppermute x30, waiting for transfers between devices, exchange(): return lax.ppermute(value, axis, pairs)  45 us
    ppermute x30, starting transfers between devices, exchange(): return lax.ppermute(value, axis, pairs)  30 us
    pallas_call x5, Pallas kernels, states(): pl.pallas_call(functools.partial(states_kernel, heads, width, group, padd...  25.8 us
    unnamed x46, local copies, waits for them, and re-layouts  14.1 us
    all_to_all x1, starting transfers between devices, on_device(): lax.all_to_all(to_owners(gates), ('z', 'y'), split_axis=0, concat_axis=0,...  5.64 us
    pallas_call x1, Pallas kernels, on_device(): pl.pallas_call(functools.partial(gates_kernel, heads, levels, padded), ou...  5.26 us
  transfers between devices with their start and end apart: 32, of which 6 were waited for; matrix products, arithmetic and copies ran while one was open for 11% of the time, Pallas kernels for 40%

profile of v1, /device:TPU:0, one launch (start us, length us, event | category | flops | bytes accessed | tf_op | source)
XLA Modules:
  0.0 206.6 jit_solution(9109423975880038170)
XLA Ops:
  0.0 4.0 %collective-permute-start.1 = (bf16[1024,128]{1,0:T(8,128)(2,1)}, bf16[1024,128]{1,0:T(8,128)(2,1)S(1)}, u32[]{:S(2)}, u32[]{:S(2)}) collective-permute-start(bf16[1024,128]{1,0:T(8,128)(2,1)} %param.8), channel_id=1, source_target_pairs={{0,16},{8,24},{16,0},{24,8},{1,17},{9,25},{17,1},{25,9},{2,18},{10... | collective-permute-start | bytes 786440 | tf_op jit(solution)/shard_map/ppermute | solution.py:221
  4.0 1.6 collective-permute-start
  5.6 1.0 copy.14
  6.6 1.0 copy.15
  7.7 8.6 %collective-permute-done.1 = bf16[1024,128]{1,0:T(8,128)(2,1)S(1)} collective-permute-done((bf16[1024,128]{1,0:T(8,128)(2,1)}, bf16[1024,128]{1,0:T(8,128)(2,1)S(1)}, u32[]{:S(2)}, u32[]{:S(2)}) %collective-permute-start.1) | collective-permute-done | bytes 262176 | tf_op jit(solution)/shard_map/ppermute | solution.py:221
  17.8 5.6 %all-to-all-start = ((f32[8,4,16,256]{3,2,1,0:T(8,128)}), f32[8,4,16,256]{3,2,1,0:T(8,128)S(1)}, u32[]{:S(2)}, u32[]{:S(2)}) async-start(f32[8,4,16,256]{3,2,1,0:T(8,128)} %bitcast.3), calls=%async_computation | async-start | bytes 1048576 | tf_op jit(solution)/shard_map/all_to_all | solution.py:295
  25.6 1.5 collective-permute-start.3
  27.1 2.0 collective-permute-start.5
  29.7 2.0 collective-permute-start.17
  32.4 18.0 %collective-permute-done.12 = bf16[1024,128]{1,0:T(8,128)(2,1)} collective-permute-done((bf16[1024,128]{1,0:T(8,128)(2,1)S(1)}, bf16[1024,128]{1,0:T(8,128)(2,1)}, u32[]{:S(2)}, u32[]{:S(2)}) %collective-permute-start.12) | collective-permute-done | bytes 262176 | tf_op jit(solution)/shard_map/ppermute | solution.py:221
  50.5 1.5 collective-permute-start.16
  52.0 3.4 %collective-permute-done.13 = bf16[1024,128]{1,0:T(8,128)(2,1)S(1)} collective-permute-done((bf16[1024,128]{1,0:T(8,128)(2,1)S(1)}, bf16[1024,128]{1,0:T(8,128)(2,1)S(1)}, u32[]{:S(2)}, u32[]{:S(2)}) %collective-permute-start.13) | collective-permute-done | bytes 262176 | tf_op jit(solution)/shard_map/ppermute | solution.py:221
  55.4 1.0 collective-permute-start.14
  57.1 1.0 constant_dynamic-update-slice_fusion.7
  58.1 2.9 %collective-permute-done.17 = bf16[1024,128]{1,0:T(8,128)(2,1)S(1)} collective-permute-done((bf16[1024,128]{1,0:T(8,128)(2,1)S(1)}, bf16[1024,128]{1,0:T(8,128)(2,1)S(1)}, u32[]{:S(2)}, u32[]{:S(2)}) %collective-permute-start.17) | collective-permute-done | bytes 262176 | tf_op jit(solution)/shard_map/ppermute | solution.py:221
  61.0 3.0 %collective-permute-start.9 = (bf16[1024,128]{1,0:T(8,128)(2,1)S(1)}, bf16[1024,128]{1,0:T(8,128)(2,1)}, u32[]{:S(2)}, u32[]{:S(2)}) collective-permute-start(bf16[1024,128]{1,0:T(8,128)(2,1)S(1)} %copy-done.11), channel_id=1, source_target_pairs={{0,16},{8,24},{16,0},{24,8},{1,17},{9,25},{17,1},{25,9},{2,18},{10... | collective-permute-start | bytes 786440 | tf_op jit(solution)/shard_map/ppermute | solution.py:221
  64.8 2.9 %convert_element_type.3 = bf16[16,8,4096]{2,1,0:T(8,128)(2,1)} convert(f32[16,8,4096]{2,1,0:T(8,128)} %param.12) | non-fusion elementwise | flops 524288 | bytes 3145728 | tf_op jit(solution)/shard_map/convert_element_type | solution.py:304
  67.7 3.6 %all-to-all-start.1 = ((bf16[8,16,4096]{2,1,0:T(8,128)(2,1)}), bf16[8,16,4096]{2,1,0:T(8,128)(2,1)S(1)}, u32[]{:S(2)}, u32[]{:S(2)}) async-start(bf16[8,16,4096]{2,1,0:T(8,128)(2,1)} %bitcast.38), calls=%async_computation.1 | async-start | bytes 2097152 | tf_op jit(solution)/shard_map/all_to_all | solution.py:303
  71.2 1.0 slice.16
  72.3 1.1 collective-permute-start.18
  73.4 1.9 collective-permute-start.4
  75.3 1.7 constant_dynamic-update-slice_fusion.11
  77.0 1.2 constant_dynamic-update-slice_fusion.5.mine_ref.my_key_ref
  78.6 1.0 collective-permute-start.6
  80.3 1.5 collective-permute-start.10
  82.5 9.4 %collective-permute-done.4 = bf16[1536,128]{1,0:T(8,128)(2,1)S(1)} collective-permute-done((bf16[1536,128]{1,0:T(8,128)(2,1)S(1)}, bf16[1536,128]{1,0:T(8,128)(2,1)S(1)}, u32[]{:S(2)}, u32[]{:S(2)}) %collective-permute-start.4) | collective-permute-done | bytes 393248 | tf_op jit(solution)/shard_map/ppermute | solution.py:221
  92.7 2.6 %collective-permute-done.10 = bf16[1024,128]{1,0:T(8,128)(2,1)S(1)} collective-permute-done((bf16[1024,128]{1,0:T(8,128)(2,1)}, bf16[1024,128]{1,0:T(8,128)(2,1)S(1)}, u32[]{:S(2)}, u32[]{:S(2)}) %collective-permute-start.10) | collective-permute-done | bytes 262176 | tf_op jit(solution)/shard_map/ppermute | solution.py:221
  96.6 0.9 copy-done.3
  97.6 2.0 pad_maximum_fusion.my_query_ref
  99.6 5.3 %gates.1 = (f32[2,128,256]{2,1,0:T(8,128)}, f32[2,128,256]{2,1,0:T(8,128)}, f32[2,128,256]{2,1,0:T(8,128)}, f32[2,128,128]{2,1,0:T(8,128)}, f32[2,1024,128]{2,1,0:T(8,128)}, /*index=5*/f32[2,1024,128]{2,1,0:T(8,128)}) custom-call(f32[8,4,16,256]{3,2,1,0:T(8,128)} %copy-done.4), custom_call_target="tpu_custom_call" | custom-call | tf_op jit(solution)/shard_map/gates/pallas_call | solution.py:319
  104.8 0.9 collective-permute-start.11
  105.7 2.6 %collective-permute-start.25 = (bf16[3072,128]{1,0:T(8,128)(2,1)}, bf16[3072,128]{1,0:T(8,128)(2,1)S(1)}, u32[]{:S(2)}, u32[]{:S(2)}) collective-permute-start(bf16[3072,128]{1,0:T(8,128)(2,1)} %pad_maximum_fusion.my_query_ref), channel_id=1, source_target_pairs={{0,4},{4,0},{1,5},{5,1},{2,6},{6,2},{3,7},{7,3},{8,12},{12,8},{9,1... | collective-permute-start | bytes 2359304 | tf_op jit(solution)/shard_map/ppermute | solution.py:221
  109.8 5.1 %states.6 = (bf16[3,16,128,128]{3,2,1,0:T(8,128)(2,1)}, f32[3,128,128]{2,1,0:T(8,128)}) custom-call(s32[3]{0:T(128)} %copy-done.15, s32[1]{0:T(128)} %bitcast.core_ref, bf16[128,32768]{1,0:T(8,128)(2,1)} %x_ref.19, bf16[3072,128]{1,0:T(8,128)(2,1)} %constant_dynamic-update-slice_fusion.mine_ref.my_key_ref, bf16[3072,128]{1,0:T(8,128)(2,1)} %copy-done.3, ...), custom_call_target="tpu_custom_call" | custom-call | flops 201326592 | bytes 6291456 | tf_op jit(solution)/shard_map/states/pallas_call | solution.py:343
  114.9 5.5 %states.5 = (bf16[4,16,128,128]{3,2,1,0:T(8,128)(2,1)}, f32[4,128,128]{2,1,0:T(8,128)}) custom-call(s32[4]{0:T(128)} %pad_add_fusion.groups_ref, s32[1]{0:T(128)} %bitcast.core_ref, bf16[128,32768]{1,0:T(8,128)(2,1)} %x_ref.19, bf16[4096,128]{1,0:T(8,128)(2,1)} %copy-done.1, bf16[4096,128]{1,0:T(8,128)(2,1)} %collective-permute-done.15.other_ref.other_key_ref, ...), custom_call_target="tpu_custom_call" | custom-call | flops 268435456 | bytes 8388608 | tf_op jit(solution)/shard_map/states/pallas_call | solution.py:343
  120.5 5.0 %states.7 = (bf16[3,16,128,128]{3,2,1,0:T(8,128)(2,1)}, f32[3,128,128]{2,1,0:T(8,128)}) custom-call(s32[3]{0:T(128)} %copy-done.14, s32[1]{0:T(128)} %bitcast.core_ref, bf16[128,32768]{1,0:T(8,128)(2,1)} %x_ref.19, bf16[3072,128]{1,0:T(8,128)(2,1)} %collective-permute-done.3.mine_ref.my_key_ref, ...), custom_call_target="tpu_custom_call" | custom-call | flops 201326592 | bytes 6291456 | tf_op jit(solution)/shard_map/states/pallas_call | solution.py:343
  125.5 5.1 %states.8 = (bf16[3,16,128,128]{3,2,1,0:T(8,128)(2,1)}, f32[3,128,128]{2,1,0:T(8,128)}) custom-call(s32[3]{0:T(128)} %copy-done.13, s32[1]{0:T(128)} %bitcast.core_ref, bf16[128,32768]{1,0:T(8,128)(2,1)} %x_ref.19, bf16[3072,128]{1,0:T(8,128)(2,1)} %copy-done.2, bf16[3072,128]{1,0:T(8,128)(2,1)} %collective-permute-done.22.other_ref.other_key_ref, ...), custom_call_target="tpu_custom_call" | custom-call | flops 201326592 | bytes 6291456 | tf_op jit(solution)/shard_map/states/pallas_call | solution.py:343
  130.6 5.1 %states.9 = (bf16[3,16,128,128]{3,2,1,0:T(8,128)(2,1)}, f32[3,128,128]{2,1,0:T(8,128)}) custom-call(s32[3]{0:T(128)} %copy-done.12, s32[1]{0:T(128)} %bitcast.core_ref, bf16[128,32768]{1,0:T(8,128)(2,1)} %x_ref.19, bf16[3072,128]{1,0:T(8,128)(2,1)} %constant_dynamic-update-slice_fusion.3.mine_ref.my_key_ref, ...), custom_call_target="tpu_custom_call" | custom-call | flops 201326592 | bytes 6291456 | tf_op jit(solution)/shard_map/states/pallas_call | solution.py:343
  135.6 3.2 %tree.1.high_ref = bf16[16,128,128]{2,1,0:T(8,128)(2,1)} custom-call(s32[16]{0:T(128)} %concatenate.31.groups_ref, f32[2,1024,128]{2,1,0:T(8,128)} %get-tuple-element.31.merge_ref, f32[4,128,128]{2,1,0:T(8,128)} %get-tuple-element.33.refs_0_, f32[3,128,128]{2,1,0:T(8,128)} %get-tuple-element.34.refs_1_, f32[3,128,128]{2,1,0:T(8,128)} %get-tuple-element.35.refs_2_, ...), custom_call_target="tpu_custom_call" | custom-call | tf_op jit(solution)/shard_map/tree/pallas_call | solution.py:380
  138.8 1.0 copy-done
  139.7 14.1 %outputs.5.refs_0_ = bf16[128,32768]{1,0:T(8,128)(2,1)} custom-call(s32[4]{0:T(128)} %pad_add_fusion.groups_ref, s32[1]{0:T(128)} %bitcast.core_ref, f32[2]{0:T(128)} %dynamic_slice.3.skip_ref, bf16[128,32768]{1,0:T(8,128)(2,1)} %x_ref.19, bf16[4096,128]{1,0:T(8,128)(2,1)} %copy-done.1, bf16[4096,128]{1,0:T(8,128)(2,1)} %collective-permute-done.15.other_ref.other_key_ref, ...), custom_call_target="tpu_custom_call" | custom-call | flops 2952790016 | bytes 8388608 | tf_op jit(solution)/shard_map/outputs/pallas_call | solution.py:397
  154.2 1.8 slice.14
  156.9 0.9 copy-done.7
  157.7 11.4 %outputs.6.refs_0_ = bf16[128,32768]{1,0:T(8,128)(2,1)} custom-call(s32[3]{0:T(128)} %copy-done.15, s32[1]{0:T(128)} %bitcast.core_ref, f32[2]{0:T(128)} %dynamic_slice.3.skip_ref, bf16[128,32768]{1,0:T(8,128)(2,1)} %x_ref.19, bf16[3072,128]{1,0:T(8,128)(2,1)} %constant_dynamic-update-slice_fusion.mine_ref.my_key_ref, ...), custom_call_target="tpu_custom_call", output_to_operand_aliasing={{}: (14, {})} | custom-call | flops 2214592512 | bytes 6291456 | tf_op jit(solution)/shard_map/outputs/pallas_call | solution.py:397
  169.1 1.0 constant_dynamic-update-slice_fusion.14
  170.4 1.0 copy-done.9
  171.4 11.6 %outputs.7.refs_0_ = bf16[128,32768]{1,0:T(8,128)(2,1)} custom-call(s32[3]{0:T(128)} %copy-done.14, s32[1]{0:T(128)} %bitcast.core_ref, f32[2]{0:T(128)} %dynamic_slice.3.skip_ref, bf16[128,32768]{1,0:T(8,128)(2,1)} %x_ref.19, bf16[3072,128]{1,0:T(8,128)(2,1)} %collective-permute-done.3.mine_ref.my_key_ref, ...), custom_call_target="tpu_custom_call", output_to_operand_aliasing={{}: (14, {})} | custom-call | flops 2214592512 | bytes 6291456 | tf_op jit(solution)/shard_map/outputs/pallas_call | solution.py:397
  183.8 11.4 %outputs.8.refs_0_ = bf16[128,32768]{1,0:T(8,128)(2,1)} custom-call(s32[3]{0:T(128)} %copy-done.13, s32[1]{0:T(128)} %bitcast.core_ref, f32[2]{0:T(128)} %dynamic_slice.3.skip_ref, bf16[128,32768]{1,0:T(8,128)(2,1)} %x_ref.19, bf16[3072,128]{1,0:T(8,128)(2,1)} %copy-done.2, ...), custom_call_target="tpu_custom_call", output_to_operand_aliasing={{}: (14, {})} | custom-call | flops 2214592512 | bytes 6291456 | tf_op jit(solution)/shard_map/outputs/pallas_call | solution.py:397
  195.2 11.4 %outputs.9 = bf16[128,32768]{1,0:T(8,128)(2,1)} custom-call(s32[3]{0:T(128)} %copy-done.12, s32[1]{0:T(128)} %bitcast.core_ref, f32[2]{0:T(128)} %dynamic_slice.3.skip_ref, bf16[128,32768]{1,0:T(8,128)(2,1)} %x_ref.19, bf16[3072,128]{1,0:T(8,128)(2,1)} %constant_dynamic-update-slice_fusion.3.mine_ref.my_key_ref, ...), custom_call_target="tpu_custom_call", output_to_operand_aliasing={{}: (14, {})} | custom-call | flops 2214592512 | bytes 6291456 | tf_op jit(solution)/shard_map/outputs/pallas_call | solution.py:397
  (93 shorter events, 14.2 us)
Async XLA Ops:
  0.0 16.3 %collective-permute-start.1 = (bf16[1024,128]{1,0:T(8,128)(2,1)}, bf16[1024,128]{1,0:T(8,128)(2,1)S(1)}, u32[]{:S(2)}, u32[]{:S(2)}) collective-permute-start(bf16[1024,128]{1,0:T(8,128)(2,1)} %param.8), channel_id=1, source_target_pairs={{0,16},{8,24},{16,0},{24,8},{1,17},{9,25},{17,1},{25,9},{2,18},{10... | collective-permute-start | bytes 786440 | tf_op jit(solution)/shard_map/ppermute | solution.py:221
  4.0 19.4 %collective-permute-start = (bf16[1024,128]{1,0:T(8,128)(2,1)}, bf16[1024,128]{1,0:T(8,128)(2,1)S(1)}, u32[]{:S(2)}, u32[]{:S(2)}) collective-permute-start(bf16[1024,128]{1,0:T(8,128)(2,1)} %param.8), channel_id=1, source_target_pairs={{0,8},{8,0},{16,24},{24,16},{1,9},{9,1},{17,25},{25,17},{2,10},{10... | collective-permute-start | bytes 786440 | tf_op jit(solution)/shard_map/ppermute | solution.py:221
  16.3 8.6 %collective-permute-start.2 = (bf16[1024,128]{1,0:T(8,128)(2,1)S(1)}, bf16[1024,128]{1,0:T(8,128)(2,1)S(1)}, u32[]{:S(2)}, u32[]{:S(2)}) collective-permute-start(bf16[1024,128]{1,0:T(8,128)(2,1)S(1)} %collective-permute-done.1), channel_id=1, source_target_pairs={{0,8},{8,0},{16,24},{24,16},{1,9},{9,1},{17,25},{25,17},{2,10},{10... | collective-permute-start | bytes 786440 | tf_op jit(solution)/shard_map/ppermute | solution.py:221
  17.8 11.3 %copy-start.10 = (bf16[1024,128]{1,0:T(8,128)(2,1)S(1)}, bf16[1024,128]{1,0:T(8,128)(2,1)}, u32[]{:S(2)}) copy-start(bf16[1024,128]{1,0:T(8,128)(2,1)} %param.8) | copy-start | bytes 786436
  17.8 11.9 %copy-start.11 = (bf16[1024,128]{1,0:T(8,128)(2,1)S(1)}, bf16[1024,128]{1,0:T(8,128)(2,1)}, u32[]{:S(2)}) copy-start(bf16[1024,128]{1,0:T(8,128)(2,1)} %param.9) | copy-start | bytes 786436
  17.8 46.9 %all-to-all-start = ((f32[8,4,16,256]{3,2,1,0:T(8,128)}), f32[8,4,16,256]{3,2,1,0:T(8,128)S(1)}, u32[]{:S(2)}, u32[]{:S(2)}) async-start(f32[8,4,16,256]{3,2,1,0:T(8,128)} %bitcast.3), calls=%async_computation | async-start | bytes 1048576 | tf_op jit(solution)/shard_map/all_to_all | solution.py:295
  23.5 33.0 %copy-start.16 = (f32[16]{0:T(128)S(1)}, f32[16]{0:T(128)}, u32[]{:S(2)}) copy-start(f32[16]{0:T(128)} %param.13) | copy-start | bytes 196
  25.6 38.4 %collective-permute-start.3 = (bf16[3072,128]{1,0:T(8,128)(2,1)}, bf16[3072,128]{1,0:T(8,128)(2,1)}, u32[]{:S(2)}, u32[]{:S(2)}) collective-permute-start(bf16[3072,128]{1,0:T(8,128)(2,1)} %constant_dynamic-update-slice_fusion.mine_ref.my_key_ref), channel_id=1, source_target_pairs={{0,2},{2,0},{1,3},{3,1},{4,6},{6,4},{5,7},{7,5},{8,10},{10,8},{9,1... | collective-permute-start | bytes 2359304 | tf_op jit(solution)/shard_map/ppermute | solution.py:221
  27.1 49.9 %collective-permute-start.5 = (bf16[3072,128]{1,0:T(8,128)(2,1)}, bf16[3072,128]{1,0:T(8,128)(2,1)S(1)}, u32[]{:S(2)}, u32[]{:S(2)}) collective-permute-start(bf16[3072,128]{1,0:T(8,128)(2,1)} %constant_dynamic-update-slice_fusion.mine_ref.my_key_ref), channel_id=1, source_target_pairs={{0,4},{4,0},{1,5},{5,1},{2,6},{6,2},{3,7},{7,3},{8,12},{12,8},{9,1... | collective-permute-start | bytes 2359304 | tf_op jit(solution)/shard_map/ppermute | solution.py:221
  29.1 21.3 %collective-permute-start.12 = (bf16[1024,128]{1,0:T(8,128)(2,1)S(1)}, bf16[1024,128]{1,0:T(8,128)(2,1)}, u32[]{:S(2)}, u32[]{:S(2)}) collective-permute-start(bf16[1024,128]{1,0:T(8,128)(2,1)S(1)} %copy-done.10), channel_id=1, source_target_pairs={{0,2},{2,0},{1,3},{3,1},{4,6},{6,4},{5,7},{7,5},{8,10},{10,8},{9,1... | collective-permute-start | bytes 786440 | tf_op jit(solution)/shard_map/ppermute | solution.py:221
  29.7 25.7 %collective-permute-start.13 = (bf16[1024,128]{1,0:T(8,128)(2,1)S(1)}, bf16[1024,128]{1,0:T(8,128)(2,1)S(1)}, u32[]{:S(2)}, u32[]{:S(2)}) collective-permute-start(bf16[1024,128]{1,0:T(8,128)(2,1)S(1)} %copy-done.10), channel_id=1, source_target_pairs={{0,4},{4,0},{1,5},{5,1},{2,6},{6,2},{3,7},{7,3},{8,12},{12,8},{9,1... | collective-permute-start | bytes 786440 | tf_op jit(solution)/shard_map/ppermute | solution.py:221
  29.7 31.3 %collective-permute-start.17 = (bf16[1024,128]{1,0:T(8,128)(2,1)S(1)}, bf16[1024,128]{1,0:T(8,128)(2,1)S(1)}, u32[]{:S(2)}, u32[]{:S(2)}) collective-permute-start(bf16[1024,128]{1,0:T(8,128)(2,1)S(1)} %copy-done.11), channel_id=1, source_target_pairs={{0,4},{4,0},{1,5},{5,1},{2,6},{6,2},{3,7},{7,3},{8,12},{12,8},{9,1... | collective-permute-start | bytes 786440 | tf_op jit(solution)/shard_map/ppermute | solution.py:221
  50.5 21.8 %collective-permute-start.16 = (bf16[1024,128]{1,0:T(8,128)(2,1)S(1)}, bf16[1024,128]{1,0:T(8,128)(2,1)}, u32[]{:S(2)}, u32[]{:S(2)}) collective-permute-start(bf16[1024,128]{1,0:T(8,128)(2,1)S(1)} %copy-done.11), channel_id=1, source_target_pairs={{0,2},{2,0},{1,3},{3,1},{4,6},{6,4},{5,7},{7,5},{8,10},{10,8},{9,1... | collective-permute-start | bytes 786440 | tf_op jit(solution)/shard_map/ppermute | solution.py:221
  55.4 18.0 %collective-permute-start.14 = (bf16[1024,128]{1,0:T(8,128)(2,1)}, bf16[1024,128]{1,0:T(8,128)(2,1)}, u32[]{:S(2)}, u32[]{:S(2)}) collective-permute-start(bf16[1024,128]{1,0:T(8,128)(2,1)} %collective-permute-done.12), channel_id=1, source_target_pairs={{0,4},{4,0},{1,5},{5,1},{2,6},{6,2},{3,7},{7,3},{8,12},{12,8},{9,1... | collective-permute-start | bytes 786440 | tf_op jit(solution)/shard_map/ppermute | solution.py:221
  56.4 52.0 %copy-start.12 = (s32[3]{0:T(128)}, s32[3]{0:T(128)S(1)}, u32[]{:S(2)}) copy-start(s32[3]{0:T(128)S(1)} %broadcast_add_fusion.3.groups_ref) | copy-start | bytes 40
  61.0 17.2 %collective-permute-start.9 = (bf16[1024,128]{1,0:T(8,128)(2,1)S(1)}, bf16[1024,128]{1,0:T(8,128)(2,1)}, u32[]{:S(2)}, u32[]{:S(2)}) collective-permute-start(bf16[1024,128]{1,0:T(8,128)(2,1)S(1)} %copy-done.11), channel_id=1, source_target_pairs={{0,16},{8,24},{16,0},{24,8},{1,17},{9,25},{17,1},{25,9},{2,18},{10... | collective-permute-start | bytes 786440 | tf_op jit(solution)/shard_map/ppermute | solution.py:221
  64.1 14.6 %collective-permute-start.8 = (bf16[1024,128]{1,0:T(8,128)(2,1)S(1)}, bf16[1024,128]{1,0:T(8,128)(2,1)}, u32[]{:S(2)}, u32[]{:S(2)}) collective-permute-start(bf16[1024,128]{1,0:T(8,128)(2,1)S(1)} %copy-done.11), channel_id=1, source_target_pairs={{0,8},{8,0},{16,24},{24,16},{1,9},{9,1},{17,25},{25,17},{2,10},{10... | collective-permute-start | bytes 786440 | tf_op jit(solution)/shard_map/ppermute | solution.py:221
  64.8 2.9 %copy-start.4 = (f32[8,4,16,256]{3,2,1,0:T(8,128)}, f32[8,4,16,256]{3,2,1,0:T(8,128)S(1)}, u32[]{:S(2)}) copy-start(f32[8,4,16,256]{3,2,1,0:T(8,128)S(1)} %all-to-all-done.gates_ref) | copy-start | bytes 1572868
  67.7 71.1 %all-to-all-start.1 = ((bf16[8,16,4096]{2,1,0:T(8,128)(2,1)}), bf16[8,16,4096]{2,1,0:T(8,128)(2,1)S(1)}, u32[]{:S(2)}, u32[]{:S(2)}) async-start(bf16[8,16,4096]{2,1,0:T(8,128)(2,1)} %bitcast.38), calls=%async_computation.1 | async-start | bytes 2097152 | tf_op jit(solution)/shard_map/all_to_all | solution.py:303
  72.3 8.1 %collective-permute-start.18 = (bf16[1024,128]{1,0:T(8,128)(2,1)S(1)}, bf16[1024,128]{1,0:T(8,128)(2,1)S(1)}, u32[]{:S(2)}, u32[]{:S(2)}) collective-permute-start(bf16[1024,128]{1,0:T(8,128)(2,1)S(1)} %collective-permute-done.17), channel_id=1, source_target_pairs={{0,2},{2,0},{1,3},{3,1},{4,6},{6,4},{5,7},{7,5},{8,10},{10,8},{9,1... | collective-permute-start | bytes 786440 | tf_op jit(solution)/shard_map/ppermute | solution.py:221
  73.4 18.5 %collective-permute-start.4 = (bf16[1536,128]{1,0:T(8,128)(2,1)S(1)}, bf16[1536,128]{1,0:T(8,128)(2,1)S(1)}, u32[]{:S(2)}, u32[]{:S(2)}) collective-permute-start(bf16[1536,128]{1,0:T(8,128)(2,1)S(1)} %slice.16), channel_id=1, source_target_pairs={{0,4},{4,0},{1,5},{5,1},{2,6},{6,2},{3,7},{7,3},{8,12},{12,8},{9,1... | collective-permute-start | bytes 1179656 | tf_op jit(solution)/shard_map/ppermute | solution.py:221
  77.0 18.3 %copy-start.2 = (bf16[3072,128]{1,0:T(8,128)(2,1)}, bf16[3072,128]{1,0:T(8,128)(2,1)S(1)}, u32[]{:S(2)}) copy-start(bf16[3072,128]{1,0:T(8,128)(2,1)S(1)} %collective-permute-done.5.mine_ref.my_key_ref) | copy-start | bytes 2359300
  77.0 19.6 %collective-permute-start.20 = (bf16[3072,128]{1,0:T(8,128)(2,1)}, bf16[3072,128]{1,0:T(8,128)(2,1)S(1)}, u32[]{:S(2)}, u32[]{:S(2)}) collective-permute-start(bf16[3072,128]{1,0:T(8,128)(2,1)} %constant_dynamic-update-slice_fusion.mine_ref.my_key_ref), channel_id=1, source_target_pairs={{0,1},{1,0},{2,3},{3,2},{4,5},{5,4},{6,7},{7,6},{8,9},{9,8},{10,11... | collective-permute-start | bytes 2359304 | tf_op jit(solution)/shard_map/ppermute | solution.py:221
  78.2 18.5 %copy-start.1 = (bf16[4096,128]{1,0:T(8,128)(2,1)}, bf16[4096,128]{1,0:T(8,128)(2,1)S(1)}, u32[]{:S(2)}) copy-start(bf16[4096,128]{1,0:T(8,128)(2,1)S(1)} %constant_dynamic-update-slice_fusion.5.mine_ref.my_key_ref) | copy-start | bytes 3145732
  78.2 26.6 %collective-permute-start.15 = (bf16[4096,128]{1,0:T(8,128)(2,1)S(1)}, bf16[4096,128]{1,0:T(8,128)(2,1)}, u32[]{:S(2)}, u32[]{:S(2)}) collective-permute-start(bf16[4096,128]{1,0:T(8,128)(2,1)S(1)} %constant_dynamic-update-slice_fusion.5.mine_ref.my_key_ref), channel_id=1, source_target_pairs={{0,1},{1,0},{2,3},{3,2},{4,5},{5,4},{6,7},{7,6},{8,9},{9,8},{10,11... | collective-permute-start | bytes 3145736 | tf_op jit(solution)/shard_map/ppermute | solution.py:221
  78.6 16.7 %collective-permute-start.6 = (bf16[1536,128]{1,0:T(8,128)(2,1)S(1)}, bf16[1536,128]{1,0:T(8,128)(2,1)S(1)}, u32[]{:S(2)}, u32[]{:S(2)}) collective-permute-start(bf16[1536,128]{1,0:T(8,128)(2,1)S(1)} %slice.17), channel_id=1, source_target_pairs={{0,2},{2,0},{1,3},{3,1},{4,6},{6,4},{5,7},{7,5},{8,10},{10,8},{9,1... | collective-permute-start | bytes 1179656 | tf_op jit(solution)/shard_map/ppermute | solution.py:221
  80.3 15.0 %collective-permute-start.10 = (bf16[1024,128]{1,0:T(8,128)(2,1)}, bf16[1024,128]{1,0:T(8,128)(2,1)S(1)}, u32[]{:S(2)}, u32[]{:S(2)}) collective-permute-start(bf16[1024,128]{1,0:T(8,128)(2,1)} %collective-permute-done.9), channel_id=1, source_target_pairs={{0,8},{8,0},{16,24},{24,16},{1,9},{9,1},{17,25},{25,17},{2,10},{10... | collective-permute-start | bytes 786440 | tf_op jit(solution)/shard_map/ppermute | solution.py:221
  91.9 13.8 %collective-permute-start.21 = (bf16[3072,128]{1,0:T(8,128)(2,1)}, bf16[3072,128]{1,0:T(8,128)(2,1)}, u32[]{:S(2)}, u32[]{:S(2)}) collective-permute-start(bf16[3072,128]{1,0:T(8,128)(2,1)} %collective-permute-done.3.mine_ref.my_key_ref), channel_id=1, source_target_pairs={{0,1},{1,0},{2,3},{3,2},{4,5},{5,4},{6,7},{7,6},{8,9},{9,8},{10,11... | collective-permute-start | bytes 2359304 | tf_op jit(solution)/shard_map/ppermute | solution.py:221
  95.3 43.5 %collective-permute-start.19 = (bf16[4096,128]{1,0:T(8,128)(2,1)}, bf16[4096,128]{1,0:T(8,128)(2,1)}, u32[]{:S(2)}, u32[]{:S(2)}) collective-permute-start(bf16[4096,128]{1,0:T(8,128)(2,1)} %constant_dynamic-update-slice_fusion.9.my_query_ref), channel_id=1, source_target_pairs={{0,1},{1,0},{2,3},{3,2},{4,5},{5,4},{6,7},{7,6},{8,9},{9,8},{10,11... | collective-permute-start | bytes 3145736 | tf_op jit(solution)/shard_map/ppermute | solution.py:221
  95.3 13.0 %collective-permute-start.22 = (bf16[3072,128]{1,0:T(8,128)(2,1)S(1)}, bf16[3072,128]{1,0:T(8,128)(2,1)}, u32[]{:S(2)}, u32[]{:S(2)}) collective-permute-start(bf16[3072,128]{1,0:T(8,128)(2,1)S(1)} %collective-permute-done.5.mine_ref.my_key_ref), channel_id=1, source_target_pairs={{0,1},{1,0},{2,3},{3,2},{4,5},{5,4},{6,7},{7,6},{8,9},{9,8},{10,11... | collective-permute-start | bytes 2359304 | tf_op jit(solution)/shard_map/ppermute | solution.py:221
  96.6 0.9 copy-start.3
  97.5 33.0 %collective-permute-start.7 = (bf16[3072,128]{1,0:T(8,128)(2,1)}, bf16[3072,128]{1,0:T(8,128)(2,1)}, u32[]{:S(2)}, u32[]{:S(2)}) collective-permute-start(bf16[3072,128]{1,0:T(8,128)(2,1)} %constant_dynamic-update-slice_fusion.3.mine_ref.my_key_ref), channel_id=1, source_target_pairs={{0,1},{1,0},{2,3},{3,2},{4,5},{5,4},{6,7},{7,6},{8,9},{9,8},{10,11... | collective-permute-start | bytes 2359304 | tf_op jit(solution)/shard_map/ppermute | solution.py:221
  104.8 49.0 %collective-permute-start.11 = (bf16[3072,128]{1,0:T(8,128)(2,1)}, bf16[3072,128]{1,0:T(8,128)(2,1)}, u32[]{:S(2)}, u32[]{:S(2)}) collective-permute-start(bf16[3072,128]{1,0:T(8,128)(2,1)} %pad_maximum_fusion.my_query_ref), channel_id=1, source_target_pairs={{0,2},{2,0},{1,3},{3,1},{4,6},{6,4},{5,7},{7,5},{8,10},{10,8},{9,1... | collective-permute-start | bytes 2359304 | tf_op jit(solution)/shard_map/ppermute | solution.py:221
  105.7 48.1 %collective-permute-start.25 = (bf16[3072,128]{1,0:T(8,128)(2,1)}, bf16[3072,128]{1,0:T(8,128)(2,1)S(1)}, u32[]{:S(2)}, u32[]{:S(2)}) collective-permute-start(bf16[3072,128]{1,0:T(8,128)(2,1)} %pad_maximum_fusion.my_query_ref), channel_id=1, source_target_pairs={{0,4},{4,0},{1,5},{5,1},{2,6},{6,2},{3,7},{7,3},{8,12},{12,8},{9,1... | collective-permute-start | bytes 2359304 | tf_op jit(solution)/shard_map/ppermute | solution.py:221
  108.3 6.6 %copy-start.14 = (s32[3]{0:T(128)}, s32[3]{0:T(128)S(1)}, u32[]{:S(2)}) copy-start(s32[3]{0:T(128)S(1)} %broadcast_add_fusion.2.groups_ref) | copy-start | bytes 40
  108.3 6.6 %copy-start.13 = (s32[3]{0:T(128)}, s32[3]{0:T(128)S(1)}, u32[]{:S(2)}) copy-start(s32[3]{0:T(128)S(1)} %broadcast_add_fusion.groups_ref) | copy-start | bytes 40
  108.4 48.5 %collective-permute-start.24 = (bf16[3072,128]{1,0:T(8,128)(2,1)}, bf16[3072,128]{1,0:T(8,128)(2,1)S(1)}, u32[]{:S(2)}, u32[]{:S(2)}) collective-permute-start(bf16[3072,128]{1,0:T(8,128)(2,1)} %pad_maximum_fusion.my_query_ref), channel_id=1, source_target_pairs={{0,1},{1,0},{2,3},{3,2},{4,5},{5,4},{6,7},{7,6},{8,9},{9,8},{10,11... | collective-permute-start | bytes 2359304 | tf_op jit(solution)/shard_map/ppermute | solution.py:221
  108.4 1.3 copy-start.15
  138.8 1.0 copy-start
  153.9 15.2 %copy-start.5 = (bf16[3072,128]{1,0:T(8,128)(2,1)}, bf16[3072,128]{1,0:T(8,128)(2,1)S(1)}, u32[]{:S(2)}) copy-start(bf16[3072,128]{1,0:T(8,128)(2,1)S(1)} %collective-permute-done.25.my_query_ref) | copy-start | bytes 2359300
  153.9 15.2 %collective-permute-start.26 = (bf16[1536,128]{1,0:T(8,128)(2,1)S(1)}, bf16[1536,128]{1,0:T(8,128)(2,1)S(1)}, u32[]{:S(2)}, u32[]{:S(2)}) collective-permute-start(bf16[1536,128]{1,0:T(8,128)(2,1)S(1)} %slice.15), channel_id=1, source_target_pairs={{0,2},{2,0},{1,3},{3,1},{4,6},{6,4},{5,7},{7,5},{8,10},{10,8},{9,1... | collective-permute-start | bytes 1179656 | tf_op jit(solution)/shard_map/ppermute | solution.py:221
  156.0 13.2 %collective-permute-start.23 = (bf16[1536,128]{1,0:T(8,128)(2,1)}, bf16[1536,128]{1,0:T(8,128)(2,1)}, u32[]{:S(2)}, u32[]{:S(2)}) collective-permute-start(bf16[1536,128]{1,0:T(8,128)(2,1)} %slice.14), channel_id=1, source_target_pairs={{0,4},{4,0},{1,5},{5,1},{2,6},{6,2},{3,7},{7,3},{8,12},{12,8},{9,1... | collective-permute-start | bytes 1179656 | tf_op jit(solution)/shard_map/ppermute | solution.py:221
  156.3 14.1 %collective-permute-start.29 = (bf16[3072,128]{1,0:T(8,128)(2,1)}, bf16[3072,128]{1,0:T(8,128)(2,1)S(1)}, u32[]{:S(2)}, u32[]{:S(2)}) collective-permute-start(bf16[3072,128]{1,0:T(8,128)(2,1)} %collective-permute-done.11.my_query_ref), channel_id=1, source_target_pairs={{0,1},{1,0},{2,3},{3,2},{4,5},{5,4},{6,7},{7,6},{8,9},{9,8},{10,11... | collective-permute-start | bytes 2359304 | tf_op jit(solution)/shard_map/ppermute | solution.py:221
  156.4 26.5 %collective-permute-start.28 = (bf16[3072,128]{1,0:T(8,128)(2,1)S(1)}, bf16[3072,128]{1,0:T(8,128)(2,1)S(1)}, u32[]{:S(2)}, u32[]{:S(2)}) collective-permute-start(bf16[3072,128]{1,0:T(8,128)(2,1)S(1)} %collective-permute-done.25.my_query_ref), channel_id=1, source_target_pairs={{0,1},{1,0},{2,3},{3,2},{4,5},{5,4},{6,7},{7,6},{8,9},{9,8},{10,11... | collective-permute-start | bytes 2359304 | tf_op jit(solution)/shard_map/ppermute | solution.py:221
  156.9 0.9 copy-start.7
  170.2 12.7 %copy-start.6 = (bf16[3072,128]{1,0:T(8,128)(2,1)}, bf16[3072,128]{1,0:T(8,128)(2,1)S(1)}, u32[]{:S(2)}) copy-start(bf16[3072,128]{1,0:T(8,128)(2,1)S(1)} %constant_dynamic-update-slice_fusion.13.my_query_ref) | copy-start | bytes 2359300
  170.2 25.0 %collective-permute-start.27 = (bf16[3072,128]{1,0:T(8,128)(2,1)S(1)}, bf16[3072,128]{1,0:T(8,128)(2,1)}, u32[]{:S(2)}, u32[]{:S(2)}) collective-permute-start(bf16[3072,128]{1,0:T(8,128)(2,1)S(1)} %constant_dynamic-update-slice_fusion.13.my_query_ref), channel_id=1, source_target_pairs={{0,1},{1,0},{2,3},{3,2},{4,5},{5,4},{6,7},{7,6},{8,9},{9,8},{10,11... | collective-permute-start | bytes 2359304 | tf_op jit(solution)/shard_map/ppermute | solution.py:221
  170.4 1.0 copy-start.9
  (1 other events, 0.9 us)

commit v2 on v0

v2 whole, which is shorter than its diff:
```python
import functools
import math

import jax
import jax.numpy as jnp
from jax import lax
from jax.experimental import pallas as pl
from jax.experimental.pallas import tpu as pltpu
from jax.sharding import PartitionSpec as P

P_SIZE = 64
N = 128
Q = 256
HALF = Q // 2
CORES = 2
NEVER = -1e30
VMEM_LIMIT = 60 * 1024 * 1024

f32 = jnp.float32
bf16 = jnp.bfloat16


def dot(a, b):
    return lax.dot_general(a, b, (((1,), (0,)), ((), ())), preferred_element_type=f32)


def exact_parts(value):
    high = value.astype(bf16)
    rest = value - high.astype(f32)
    middle = rest.astype(bf16)
    low = (rest - middle.astype(f32)).astype(bf16)
    return high, middle, low


def gates_kernel(heads, levels, padded, gates_ref, weight_ref, cum_ref, offset_ref, decay_ref, merge_ref,
                 log_scratch):
    shards, _, span_rows, _ = gates_ref.shape
    spans = shards * span_rows
    upper = (
        lax.broadcasted_iota(jnp.int32, (Q, Q), 0) <= lax.broadcasted_iota(jnp.int32, (Q, Q), 1)
    ).astype(f32).astype(bf16)
    chunk = min(spans, 64)
    for head in range(heads):
        for shard in range(shards):
            rows = pl.ds(shard * span_rows, span_rows)
            gate = gates_ref[shard, 2 * head]
            step = gates_ref[shard, 2 * head + 1]
            high, middle, low = exact_parts(gate)
            cumulative = dot(high, upper) + dot(middle, upper) + dot(low, upper)
            span_log = cumulative[:, Q - 1 :]
            cum_ref[head, rows, :] = cumulative
            offset_ref[head, rows, :] = cumulative - jnp.log(step)
            weight_ref[head, rows, :] = jnp.exp(span_log - cumulative) * step
            log_scratch[rows, :] = jnp.broadcast_to(span_log, (span_rows, N))
        high, middle, low = exact_parts(log_scratch[...])

        def some_spans(at, carry):
            first = at * chunk
            size = (chunk * padded, spans)
            row = lax.broadcasted_iota(jnp.int32, size, 0)
            span = first + row // padded
            level = row % padded
            other = lax.broadcasted_iota(jnp.int32, size, 1)
            out_rows = pl.ds(pl.multiple_of(first * padded, chunk * padded), chunk * padded)
            bit = jnp.maximum(level - 1, 0)
            before = (other >= (span >> bit) << bit) & (other < span)
            before = before.astype(f32).astype(bf16)
            decay = dot(before, high) + dot(before, middle) + dot(before, low)
            has_bit = ((span >> bit) & 1)[:, :1] == 1
            decay_ref[head, out_rows, :] = jnp.where(has_bit, decay, NEVER)
            right = (other > span - (1 << bit)) & (other <= span)
            right = right.astype(f32).astype(bf16)
            merge_ref[head, out_rows, :] = jnp.exp(
                dot(right, high) + dot(right, middle) + dot(right, low)
            )
            return carry

        lax.fori_loop(0, spans // chunk, some_spans, 0)


def pick_set(step, starts, values):
    value = values[0]
    for start, other in zip(starts[1:], values[1:]):
        value = jnp.where(step >= start, other, value)
    return value


def pick(core, step, starts, pairs, local, group):
    half = group // CORES
    rows = slice(local % half * Q, (local % half + 1) * Q)
    mine = core == local // half
    return pick_set(step, starts, [jnp.where(mine, my_ref[rows, :], other_ref[rows, :]) for my_ref, other_ref in pairs])


def scaled(value, rows, width):
    parts = [value[head * width : (head + 1) * width] * row for head, row in enumerate(rows)]
    return jnp.concatenate(parts, axis=0) if len(parts) > 1 else parts[0]


def merge_blocks(left, right, merge_ref, row, width):
    return scaled(left, [merge_ref[head, row : row + 1, :] for head in range(merge_ref.shape[0])], width) + right


def states_kernel(heads, width, group, padded, starts, groups_ref, core_ref, x_ref, weight_ref, merge_ref, *refs):
    *key_refs, low_ref, total_ref = refs
    pairs = list(zip(key_refs[::2], key_refs[1::2]))
    kept = {}
    for local in range(group):
        columns = slice(local * Q, (local + 1) * Q)
        weights = [weight_ref[head, local : local + 1, :] for head in range(heads)]
        weighted = scaled(x_ref[:, columns].astype(f32), weights, width).astype(bf16)
        state = dot(weighted, pick(core_ref[0], pl.program_id(0), starts, pairs, local, group))
        bit = 0
        while local >> bit & 1:
            state = merge_blocks(kept[bit], state, merge_ref, local * padded + bit + 1, width)
            bit += 1
        kept[bit] = state
        if local < group - 1:
            low_ref[local] = state.astype(bf16)
    total_ref[...] = state


def tree_kernel(width, group, padded, groups_ref, merge_ref, *refs):
    *total_refs, high_ref, order_ref = refs
    steps = order_ref.shape[0]
    low_bits = group.bit_length() - 1
    at = 0
    for total_ref in total_refs:
        for slot in range(total_ref.shape[0]):
            order_ref[groups_ref[at]] = total_ref[slot]
            at += 1
    kept = {}
    for step in range(steps):
        state = order_ref[step]
        bit = 0
        while step >> bit & 1:
            row = ((step + 1) * group - 1) * padded + low_bits + bit + 1
            state = merge_blocks(kept[bit], state, merge_ref, row, width)
            bit += 1
        kept[bit] = state
        high_ref[step] = state.astype(bf16)


def outputs_kernel(heads, width, group, bits, padded, starts, groups_ref, core_ref, skip_ref, x_ref, high_ref,
                   cum_ref, offset_ref, decay_ref, level_ref, *refs):
    *set_refs, out_ref, query_ref, total_ref, factor_ref, score_ref, mixing_ref = refs
    set_refs = [set_refs[5 * at : 5 * at + 5] for at in range(len(starts))]
    key_pairs = [refs[0:2] for refs in set_refs]
    query_pairs = [refs[2:4] for refs in set_refs]
    low_refs = [refs[4] for refs in set_refs]
    at = pl.program_id(0)
    step = groups_ref[at]
    low_bits = group.bit_length() - 1
    levels = bits + 1
    causal = lax.broadcasted_iota(jnp.int32, (HALF, HALF), 0) <= lax.broadcasted_iota(
        jnp.int32, (HALF, HALF), 1
    )
    head_rows = [slice(head * width, (head + 1) * width) for head in range(heads)]
    offsets = [jnp.transpose(offset_ref[head]) for head in range(heads)]

    @pl.when(at == 0)
    def _():
        mixing_ref[:, :, HALF:, :HALF] = jnp.zeros((2, heads, HALF, HALF), bf16)

    def span_columns(local):
        return slice(local * Q, (local + 1) * Q)

    for local in range(group):
        columns = span_columns(local)
        query_ref[:, columns] = jnp.transpose(pick(core_ref[0], at, starts, query_pairs, local, group))
        weights = level_ref[0, :, columns].astype(f32)
        for head in range(heads):
            decay = decay_ref[head, local * padded : local * padded + levels, :]
            decay = jnp.concatenate([decay] * (Q // N), axis=1)
            growth = jnp.exp(cum_ref[head, local : local + 1, :] + decay)
            factor_ref[head, :levels, columns] = weights[head * levels : (head + 1) * levels] * growth
    total_ref[...] = jnp.zeros_like(total_ref)

    def weigh(part, bit, columns):
        return [part[rows] * factor_ref[head, bit + 1 : bit + 2, columns] for head, rows in enumerate(head_rows)]

    for bit in range(low_bits, bits):
        place = bit - low_bits

        @pl.when(((step >> place) & 1) == 1)
        def _(bit=bit, place=place):
            state = high_ref[(step >> place << place) - 1]
            for local in range(group):
                columns = span_columns(local)
                terms = weigh(dot(state, query_ref[:, columns]), bit, columns)
                for rows, term in zip(head_rows, terms):
                    total_ref[rows, columns] += term

    def score(local):
        slot = local % 2
        columns = span_columns(local)
        keys = pick(core_ref[0], at, starts, key_pairs, local, group)
        upper = dot(keys[:HALF], query_ref[:, columns])
        score_ref[slot, :HALF, :HALF] = jnp.where(causal, upper[:, :HALF], 0.0)
        score_ref[slot, :HALF, HALF:] = upper[:, HALF:]
        lower = dot(keys[HALF:], query_ref[:, columns][:, HALF:])
        score_ref[slot, HALF:, HALF:] = jnp.where(causal, lower, 0.0)

    def mix(local):
        slot = local % 2
        for head in range(heads):
            left = cum_ref[head, local : local + 1, :HALF]
            right = cum_ref[head, local : local + 1, HALF:]
            column = offsets[head][:, local : local + 1]
            upper = jnp.broadcast_to(column[:HALF], (HALF, HALF))
            lower = jnp.broadcast_to(column[HALF:], (HALF, HALF))
            mixing_ref[slot, head, :HALF, :HALF] = (
                score_ref[slot, :HALF, :HALF] * jnp.exp(jnp.minimum(left - upper, 64.0))
            ).astype(bf16)
            mixing_ref[slot, head, :HALF, HALF:] = (
                score_ref[slot, :HALF, HALF:] * jnp.exp(right - upper)
            ).astype(bf16)
            mixing_ref[slot, head, HALF:, HALF:] = (
                score_ref[slot, HALF:, HALF:] * jnp.exp(jnp.minimum(right - lower, 64.0))
            ).astype(bf16)

    def level_parts(local):
        columns = span_columns(local)
        sums = [total_ref[rows, columns] for rows in head_rows]
        for bit in range(low_bits):
            if local >> bit & 1:
                slot = ((local >> bit) << bit) - 1
                state = pick_set(at, starts, [low_ref[slot] for low_ref in low_refs])
                terms = weigh(dot(state, query_ref[:, columns]), bit, columns)
                sums = [left + right for left, right in zip(sums, terms)]
        return sums

    def finish(local, sums):
        slot = local % 2
        columns = span_columns(local)
        own = level_ref[0, :, columns].astype(f32)
        for head, rows in enumerate(head_rows):
            values = x_ref[rows, columns]
            result = dot(values, mixing_ref[slot, head]) * own[head * levels : head * levels + 1]
            result += skip_ref[head] * values.astype(f32) + sums[head]
            out_ref[rows, columns] = result.astype(bf16)

    score(0)
    for local in range(group):
        sums = level_parts(local)
        if local + 1 < group:
            score(local + 1)
        mix(local)
        finish(local, sums)


def exchange(value, axis, distance):
    pairs = [(place, place ^ distance) for place in range(lax.axis_size(axis))]
    return lax.ppermute(value, axis, pairs)


def along_z(own):
    pieces = [own]
    for distance in range(1, lax.axis_size("z")):
        low = distance & -distance
        pieces.append(exchange(pieces[distance ^ low], "z", low))
    return pieces[1:]


def places():
    both = [(y, x) for y in range(lax.axis_size("y")) for x in range(lax.axis_size("x"))]
    return sorted(both, key=lambda place: ((place[0] > 0) + (place[1] > 0), place))


def straight(piece):
    near = {(0, 0): piece}
    for y, x in places():
        if (y > 0) != (x > 0):
            near[y, x] = exchange(piece, "x", x) if x else exchange(piece, "y", y)
    return near


def diagonal(near, by_x, by_y):
    far = {}
    for y, x in places():
        if y and x:
            parts = []
            if by_x is not None:
                parts.append(exchange(near[0, x][by_x], "y", y))
            if by_y is not None:
                parts.append(exchange(near[y, 0][by_y], "x", x))
            far[y, x] = parts
    return far


def join(parts):
    return jnp.concatenate(parts, axis=0) if len(parts) > 1 else parts[0]


def with_core(piece):
    return piece, exchange(piece, "core", 1)


def after(value, *others):
    return lax.optimization_barrier((value, *others))[0]


def on_device(x_heads, b_proj, c_proj, log_gate, step_size, level_weight, skip):
    rows, tokens = x_heads.shape
    head_count, tok_dev = log_gate.shape
    levels = level_weight.shape[1]
    bits = levels - 1
    shards = lax.axis_size(("z", "y"))
    span_rows = tok_dev // Q
    spans = tokens // Q
    heads = max(rows // P_SIZE, 1)
    width = rows // heads
    sharing = P_SIZE // width
    block = b_proj.shape[0]
    group = CORES * block // Q
    padded = -(-levels // 8) * 8
    steps = spans // group
    per_shard = span_rows // group

    def to_owners(value):
        value = jnp.repeat(value, sharing, axis=0) if sharing > 1 else value
        value = value.reshape((shards, heads) + value.shape[1:])
        return value.reshape((shards, -1) + value.shape[3:])

    gates = jnp.stack(
        [log_gate.reshape(head_count, span_rows, Q), step_size.reshape(head_count, span_rows, Q)], axis=1
    )
    gates = lax.all_to_all(to_owners(gates), ("z", "y"), split_axis=0, concat_axis=0, tiled=True)
    first_head = lax.axis_index(("z", "y")) * rows // P_SIZE
    own_skip = lax.dynamic_slice_in_dim(skip, first_head, heads, 0)
    core = lax.axis_index("core").astype(jnp.int32).reshape(1)

    def group_ids(place, z=None):
        z = lax.axis_index("z") ^ jnp.arange(1, lax.axis_size("z")) if z is None else z
        y = lax.axis_index("y") ^ place[0]
        x = lax.axis_index("x") ^ place[1]
        return ((z * lax.axis_size("y") + y) * lax.axis_size("x") + x).astype(jnp.int32)

    params = pltpu.CompilerParams(vmem_limit_bytes=VMEM_LIMIT)
    key_near = straight(b_proj)
    key_line = along_z(b_proj)
    query_near = straight(c_proj)
    crossed = [near[place] for near in (key_near, query_near) for place in places() if place in near and any(place)]
    everything = slice(None)
    key_near.update({place: join(parts) for place, parts in diagonal(key_near, everything, None).items()})
    query_near.update({place: join(parts) for place, parts in diagonal(query_near, None, everything).items()})
    query_line = along_z(after(c_proj, *key_line))
    keys_here = with_core(join([key_near[place] for place in places()]))
    queries_here = with_core(join([query_near[place] for place in places()]))

    params = pltpu.CompilerParams(vmem_limit_bytes=VMEM_LIMIT)
    weight, cumulative, offset, decay, merge = pl.pallas_call(
        functools.partial(gates_kernel, heads, levels, padded),
        out_shape=[jax.ShapeDtypeStruct((heads, spans, Q), f32)] * 3
        + [jax.ShapeDtypeStruct((heads, spans * padded, N), f32)] * 2,
        scratch_shapes=[pltpu.VMEM((spans, N), f32)],
        compiler_params=params,
        name="gates",
    )(gates)
    weight, cumulative, offset = [v.reshape(heads, steps, group, Q) for v in (weight, cumulative, offset)]
    level_rows = lax.all_to_all(
        to_owners(after(level_weight, gates).astype(bf16)), ("z", "y"), split_axis=0, concat_axis=0, tiled=True
    )

    x_spec = pl.BlockSpec((rows, group * Q), lambda i, ids, *_: (0, ids[i]))
    span_spec = pl.BlockSpec((heads, None, group, Q), lambda i, ids, *_: (0, ids[i], 0, 0))
    level_spec = pl.BlockSpec((heads, group * padded, N), lambda i, ids, *_: (0, ids[i], 0))
    low_slots = max(group - 1, 1)
    vmem = pl.BlockSpec(memory_space=pltpu.VMEM)

    def within(start, count, base, trailing):
        return lambda i, *_: (jnp.clip(i - start, 0, count - 1) + base,) + (0,) * trailing

    def first_steps(id_lists):
        return [sum(ids.shape[0] for ids in id_lists[:at]) for at in range(len(id_lists))]

    totals, all_ids = [], []

    def states(sets):
        starts = first_steps([ids for ids, _ in sets])
        ids = join([ids for ids, _ in sets])
        count = ids.shape[0]
        key_specs = [
            pl.BlockSpec((block, N), within(start, own.shape[0], 0, 1)) for start, (own, _) in zip(starts, sets)
        ]
        low, total = pl.pallas_call(
            functools.partial(states_kernel, heads, width, group, padded, starts),
            grid_spec=pltpu.PrefetchScalarGridSpec(
                num_scalar_prefetch=2,
                grid=(count,),
                in_specs=[x_spec, span_spec, level_spec] + [spec for spec in key_specs for _ in range(CORES)],
                out_specs=[
                    pl.BlockSpec((None, low_slots, rows, N), lambda i, *_: (i, 0, 0, 0)),
                    pl.BlockSpec((None, rows, N), lambda i, *_: (i, 0, 0)),
                ],
            ),
            out_shape=[
                jax.ShapeDtypeStruct((count, low_slots, rows, N), bf16),
                jax.ShapeDtypeStruct((count, rows, N), f32),
            ],
            compiler_params=params,
            cost_estimate=pl.CostEstimate(
                flops=2 * rows * count * group * Q * N,
                bytes_accessed=4 * count * group * Q * (rows + N),
                transcendentals=0,
            ),
            name="states",
        )(ids, core, x_heads, weight, merge, *[key for _, keys in sets for key in keys])
        totals.append(total)
        all_ids.append(ids)
        return [(low, start) for start in starts]

    def outputs(sets, out):
        starts = first_steps([ids for ids, *_ in sets])
        ids = join([ids for ids, *_ in sets])
        count = ids.shape[0]
        tokens_here = count * group * Q
        set_specs, operands = [], []
        for start, (own, keys, queries, (low, base)) in zip(starts, sets):
            set_specs += [pl.BlockSpec((block, N), within(start, own.shape[0], 0, 1))] * (2 * CORES)
            set_specs.append(pl.BlockSpec((None, low_slots, rows, N), within(start, own.shape[0], base, 3)))
            operands += [*keys, *queries, low]
        before = [] if out is None else [out]
        fixed = [
            pl.BlockSpec(memory_space=pltpu.SMEM),
            x_spec,
            vmem,
            span_spec,
            span_spec,
            level_spec,
            pl.BlockSpec(
                (1, heads * levels, group * Q),
                lambda i, ids, *_: (ids[i] // per_shard, 0, ids[i] % per_shard),
            ),
        ]

        def kernel(*refs):
            last = 2 + len(fixed) + len(set_specs)
            outputs_kernel(
                heads, width, group, bits, padded, starts, *refs[:last], *refs[last + len(before) :]
            )

        return pl.pallas_call(
            kernel,
            grid_spec=pltpu.PrefetchScalarGridSpec(
                num_scalar_prefetch=2,
                grid=(count,),
                in_specs=fixed + set_specs + [pl.BlockSpec(memory_space=pl.ANY)] * len(before),
                out_specs=x_spec,
                scratch_shapes=[
                    pltpu.VMEM((N, group * Q), bf16),
                    pltpu.VMEM((rows, group * Q), f32),
                    pltpu.VMEM((heads, padded, group * Q), f32),
                    pltpu.VMEM((2, Q, Q), f32),
                    pltpu.VMEM((2, heads, Q, Q), bf16),
                ],
            ),
            out_shape=jax.ShapeDtypeStruct((rows, tokens), bf16),
            input_output_aliases={2 + len(fixed) + len(set_specs): 0} if before else {},
            compiler_params=params,
            cost_estimate=pl.CostEstimate(
                flops=2 * tokens_here * (Q * N + rows * Q + bits * rows * N),
                bytes_accessed=4 * tokens_here * (rows + N),
                transcendentals=heads * tokens_here * Q,
            ),
            name="outputs",
        )(ids, core, own_skip, x_heads, high, cumulative, offset, decay, level_rows, *operands, *before)

    here = join([group_ids(place, lax.axis_index("z").reshape(1)) for place in places()])
    one = (0, 0)
    sides = [place for place in places() if (place[0] > 0) != (place[1] > 0)]
    corners = [place for place in places() if place[0] and place[1]]
    far_ids = {place: group_ids(place) for place in places()}
    lows = {}
    if key_line:
        cut = block * ((len(key_line) + 1) // 3)
        by_x, by_y = slice(0, cut), slice(cut, None)
        key_far = straight(after(join(key_line), *crossed))
        keys_far = {one: with_core(key_far[one])}
        low_here, lows[one] = states([(here, keys_here), (far_ids[one], keys_far[one])])
        query_own = join(query_line)
        ready = (totals[0], query_own, queries_here[0])
        query_far = straight(after(query_own, *[key_far[place] for place in sides]))
        if sides:
            tied = {place: after(key_far[place], *ready) for place in sides}
            parts = diagonal(tied, by_x, by_y)
            keys_far.update({place: with_core(key_far[place]) for place in sides})
            lows.update(zip(sides, states([(far_ids[place], keys_far[place]) for place in sides])))
            if corners:
                joined = {place: join([after(part, totals[1]) for part in parts[place]]) for place in corners}
                keys_far.update({place: with_core(joined[place]) for place in corners})
                lows.update(zip(corners, states([(far_ids[place], keys_far[place]) for place in corners])))
    else:
        (low_here,) = states([(here, keys_here)])

    high = pl.pallas_call(
        functools.partial(tree_kernel, width, group, padded),
        grid_spec=pltpu.PrefetchScalarGridSpec(
            num_scalar_prefetch=1,
            in_specs=[vmem] * (1 + len(totals)),
            out_specs=vmem,
            scratch_shapes=[pltpu.VMEM((steps, rows, N), f32)],
        ),
        out_shape=jax.ShapeDtypeStruct((steps, rows, N), bf16),
        compiler_params=params,
        name="tree",
    )(join(all_ids), merge, *totals)

    out = outputs([(here, keys_here, queries_here, low_here)], None)
    if key_line:
        tied = {place: after(query_far[place], out) for place in sides}
        parts = diagonal(tied, by_x, by_y)
        queries_far = {place: with_core(query_far[place] if place == one else tied[place]) for place in [one] + sides}

        def far_sets(some):
            return [(far_ids[place], keys_far[place], queries_far[place], lows[place]) for place in some]

        early = [one] + sides[: len(sides) // 2]
        late = sides[len(sides) // 2 :]
        out = outputs(far_sets(early), out)
        for place in corners:
            queries_far[place] = with_core(join([after(part, out) for part in parts[place]]))
        if late or corners:
            out = outputs(far_sets(late + corners), out)
    return out


def solution(mesh):
    x = mesh.shape["head"] // CORES
    y = math.gcd(mesh.shape["seq"], x)
    z = mesh.shape["seq"] // y
    split_mesh = jax.sharding.Mesh(mesh.devices.reshape(z, y, x, CORES), ("z", "y", "x", "core"))
    seq = ("z", "y")
    head = ("x", "core")
    in_specs = (
        P((*head, *seq), None),
        P((*seq, *head), None),
        P((*seq, *head), None),
        P(head, seq),
        P(head, seq),
        P(head, None, seq),
        P(head),
    )
    out_specs = P((*head, *seq), None)
    return jax.shard_map(
        on_device, mesh=split_mesh, in_specs=in_specs, out_specs=out_specs, check_vma=False
    )
```

time: 202 us -> 176 us (0.87)
  waiting for transfers between devices: 68.2 us -> 20.4 us
  starting transfers between devices: 28.8 us -> 39.9 us
  Pallas kernels: 75.6 us -> 83.6 us
    ppermute x22 -> x30, waiting for transfers between devices: 68.2 us -> 20.4 us  [exchange(): return lax.ppermute(value, axis, pairs)]
    ppermute x22 -> x30, starting transfers between devices: 20.8 us -> 29.9 us  [exchange(): return lax.ppermute(value, axis, pairs)]
    pallas_call x8 -> x6, Pallas kernels: 67.2 us -> 75.2 us  [the longest x3 54.8 us: outputs(): pl.pallas_call(kernel, grid_spec=pltpu.PrefetchScalarGridSpec(num_scalar_...]
    unnamed x30 -> x48, local copies, waits for them, and re-layouts: 13.1 us -> 17.4 us
    slice x4, local copies, waits for them, and re-layouts: 4.64 us -> 1.76 us  [the longest x2 1.69 us: diagonal(): parts.append(exchange(near[0, x][by_x], 'y', y))]
    all_to_all x1, starting transfers between devices: 3.49 us -> 5.57 us  [on_device(): lax.all_to_all(to_owners(gates), ('z', 'y'), split_axis=0, concat_axis=0,...]
    concatenate x4 -> x7, local copies, waits for them, and re-layouts: 5.19 us -> 4.55 us  [join(): return jnp.concatenate(parts, axis=0) if len(parts) > 1 else parts[0]]
  transfers between devices with their start and end apart: 24 -> 32, of which waited for: 10 -> 6; matrix products, arithmetic and copies ran while one was open for 13% -> 15% of each run, Pallas kernels for 32% -> 35%
where the time goes in v2:
time: 176 us; the launch traced here: 175 us
  Pallas kernels  83.6 us (48%)
  starting transfers between devices  39.9 us (23%)
  local copies, waits for them, and re-layouts  24.3 us (14%)
  waiting for transfers between devices  20.4 us (12%)
  other arithmetic  6.04 us (3%)
    pallas_call x3, Pallas kernels, outputs(): pl.pallas_call(kernel, grid_spec=pltpu.PrefetchScalarGridSpec(num_scalar_...  54.8 us
    ppermute x30, starting transfers between devices, exchange(): return lax.ppermute(value, axis, pairs)  29.9 us
    ppermute x30, waiting for transfers between devices, exchange(): return lax.ppermute(value, axis, pairs)  20.4 us
    pallas_call x3, Pallas kernels, states(): pl.pallas_call(functools.partial(states_kernel, heads, width, group, padd...  20.4 us
    unnamed x48, local copies, waits for them, and re-layouts  17.4 us
    all_to_all x1, starting transfers between devices, on_device(): lax.all_to_all(to_owners(gates), ('z', 'y'), split_axis=0, concat_axis=0,...  5.57 us
    pallas_call x1, Pallas kernels, on_device(): pl.pallas_call(functools.partial(gates_kernel, heads, levels, padded), ou...  5.26 us
    concatenate x7, local copies, waits for them, and re-layouts, join(): return jnp.concatenate(parts, axis=0) if len(parts) > 1 else parts[0]  4.55 us
  transfers between devices with their start and end apart: 32, of which 6 were waited for; matrix products, arithmetic and copies ran while one was open for 15% of the time, Pallas kernels for 35%

profile of v2, /device:TPU:0, one launch (start us, length us, event | category | flops | bytes accessed | tf_op | source)
XLA Modules:
  0.0 174.7 jit_solution(17692523601265223444)
XLA Ops:
  0.0 4.0 %collective-permute-start.5 = (bf16[1024,128]{1,0:T(8,128)(2,1)}, bf16[1024,128]{1,0:T(8,128)(2,1)S(1)}, u32[]{:S(2)}, u32[]{:S(2)}) collective-permute-start(bf16[1024,128]{1,0:T(8,128)(2,1)} %param.8), channel_id=1, source_target_pairs={{0,16},{8,24},{16,0},{24,8},{1,17},{9,25},{17,1},{25,9},{2,18},{10... | collective-permute-start | bytes 786440 | tf_op jit(solution)/shard_map/ppermute | solution.py:254
  4.0 1.5 collective-permute-start
  5.5 1.6 collective-permute-start.4
  7.1 1.5 collective-permute-start.1
  9.1 1.0 copy.12
  10.2 1.1 copy.13
  11.3 5.1 %collective-permute-done.5 = bf16[1024,128]{1,0:T(8,128)(2,1)S(1)} collective-permute-done((bf16[1024,128]{1,0:T(8,128)(2,1)}, bf16[1024,128]{1,0:T(8,128)(2,1)S(1)}, u32[]{:S(2)}, u32[]{:S(2)}) %collective-permute-start.5) | collective-permute-done | bytes 262176 | tf_op jit(solution)/shard_map/ppermute | solution.py:254
  17.0 0.8 pad_maximum_fusion.1
  17.9 5.6 %all-to-all-start = ((f32[8,4,16,256]{3,2,1,0:T(8,128)}), f32[8,4,16,256]{3,2,1,0:T(8,128)S(1)}, u32[]{:S(2)}, u32[]{:S(2)}) async-start(f32[8,4,16,256]{3,2,1,0:T(8,128)} %bitcast.7), calls=%async_computation | async-start | bytes 1048576 | tf_op jit(solution)/shard_map/all_to_all | solution.py:328
  24.2 1.4 collective-permute-start.7
  25.6 1.7 constant_dynamic-update-slice_fusion.2
  27.3 2.0 %collective-permute-start.2 = (bf16[1024,128]{1,0:T(8,128)(2,1)}, bf16[1024,128]{1,0:T(8,128)(2,1)S(1)}, u32[]{:S(2)}, u32[]{:S(2)}) collective-permute-start(bf16[1024,128]{1,0:T(8,128)(2,1)} %collective-permute-done), channel_id=1, source_target_pairs={{0,4},{4,0},{1,5},{5,1},{2,6},{6,2},{3,7},{7,3},{8,12},{12,8},{9,1... | collective-permute-start | bytes 786440 | tf_op jit(solution)/shard_map/ppermute | solution.py:254
  29.9 1.0 pad_maximum_fusion.refs_2_.refs_9_
  31.0 1.9 %collective-permute-done.7 = bf16[1024,128]{1,0:T(8,128)(2,1)S(1)} collective-permute-done((bf16[1024,128]{1,0:T(8,128)(2,1)S(1)}, bf16[1024,128]{1,0:T(8,128)(2,1)S(1)}, u32[]{:S(2)}, u32[]{:S(2)}) %collective-permute-start.7) | collective-permute-done | bytes 262176 | tf_op jit(solution)/shard_map/ppermute | solution.py:254
  32.8 2.6 %collective-permute-start.12 = (bf16[3072,128]{1,0:T(8,128)(2,1)S(1)}, bf16[3072,128]{1,0:T(8,128)(2,1)S(1)}, u32[]{:S(2)}, u32[]{:S(2)}) collective-permute-start(bf16[3072,128]{1,0:T(8,128)(2,1)S(1)} %pad_maximum_fusion.refs_2_.refs_9_), channel_id=1, source_target_pairs={{0,4},{4,0},{1,5},{5,1},{2,6},{6,2},{3,7},{7,3},{8,12},{12,8},{9,1... | collective-permute-start | bytes 2359304 | tf_op jit(solution)/shard_map/ppermute | solution.py:254
  35.5 1.4 collective-permute-start.10
  36.9 1.7 constant_dynamic-update-slice_fusion.1
  38.5 2.4 %collective-permute-start.15 = (bf16[1024,128]{1,0:T(8,128)(2,1)S(1)}, bf16[1024,128]{1,0:T(8,128)(2,1)}, u32[]{:S(2)}, u32[]{:S(2)}) collective-permute-start(bf16[1024,128]{1,0:T(8,128)(2,1)S(1)} %copy-done.13), channel_id=1, source_target_pairs={{0,16},{8,24},{16,0},{24,8},{1,17},{9,25},{17,1},{25,9},{2,18},{10... | collective-permute-start | bytes 786440 | tf_op jit(solution)/shard_map/ppermute | solution.py:254
  41.6 0.7 constant_dynamic-update-slice_fusion.10
  42.9 6.4 %collective-permute-done.15 = bf16[1024,128]{1,0:T(8,128)(2,1)} collective-permute-done((bf16[1024,128]{1,0:T(8,128)(2,1)S(1)}, bf16[1024,128]{1,0:T(8,128)(2,1)}, u32[]{:S(2)}, u32[]{:S(2)}) %collective-permute-start.15) | collective-permute-done | bytes 262176 | tf_op jit(solution)/shard_map/ppermute | solution.py:254
  50.2 1.7 constant_dynamic-update-slice_fusion.9
  51.9 1.7 constant_dynamic-update-slice_fusion.8
  53.6 3.0 %collective-permute-done.14 = bf16[1024,128]{1,0:T(8,128)(2,1)} collective-permute-done((bf16[1024,128]{1,0:T(8,128)(2,1)S(1)}, bf16[1024,128]{1,0:T(8,128)(2,1)}, u32[]{:S(2)}, u32[]{:S(2)}) %collective-permute-start.14) | collective-permute-done | bytes 262176 | tf_op jit(solution)/shard_map/ppermute | solution.py:254
  57.9 1.7 constant_dynamic-update-slice_fusion.6
  59.6 2.9 %convert_element_type.3 = bf16[16,8,4096]{2,1,0:T(8,128)(2,1)} convert(f32[16,8,4096]{2,1,0:T(8,128)} %param.12) | non-fusion elementwise | flops 524288 | bytes 3145728 | tf_op jit(solution)/shard_map/convert_element_type | solution.py:362
  62.5 4.4 %all-to-all-start.1 = ((bf16[8,16,4096]{2,1,0:T(8,128)(2,1)}), bf16[8,16,4096]{2,1,0:T(8,128)(2,1)S(1)}, u32[]{:S(2)}, u32[]{:S(2)}) async-start(bf16[8,16,4096]{2,1,0:T(8,128)(2,1)} %bitcast.22), calls=%async_computation.1 | async-start | bytes 2097152 | tf_op jit(solution)/shard_map/all_to_all | solution.py:361
  66.9 1.7 constant_dynamic-update-slice_fusion.5
  68.6 5.3 %gates.1 = (f32[2,128,256]{2,1,0:T(8,128)}, f32[2,128,256]{2,1,0:T(8,128)}, f32[2,128,256]{2,1,0:T(8,128)}, f32[2,1024,128]{2,1,0:T(8,128)}, f32[2,1024,128]{2,1,0:T(8,128)}) custom-call(f32[8,4,16,256]{3,2,1,0:T(8,128)} %copy-done.7), custom_call_target="tpu_custom_call" | custom-call | tf_op jit(solution)/shard_map/gates/pallas_call | solution.py:352
  73.8 1.7 constant_dynamic-update-slice_fusion.4.refs_11_
  75.5 8.3 %states.3 = (bf16[7,7,128,128]{3,2,1,0:T(8,128)(2,1)}, f32[7,128,128]{2,1,0:T(8,128)}) custom-call(s32[7]{0:T(128)} %concatenate.40.groups_ref, s32[1]{0:T(128)} %bitcast.core_ref.refs_1_, bf16[128,32768]{1,0:T(8,128)(2,1)} %refs_3_.5, f32[2,16,8,256]{3,2,1,0:T(8,128)} %bitcast.29, f32[2,1024,128]{2,1,0:T(8,128)} %get-tuple-element.28.merge_ref, ...), custom_call_target="tpu_custom_call" | custom-call | flops 469762048 | bytes 14680064 | tf_op jit(solution)/shard_map/states/pallas_call | solution.py:386
  83.9 1.1 collective-permute-start.19
  85.8 2.0 %collective-permute-start.18 = (bf16[1024,128]{1,0:T(8,128)(2,1)}, bf16[1024,128]{1,0:T(8,128)(2,1)S(1)}, u32[]{:S(2)}, u32[]{:S(2)}) collective-permute-start(bf16[1024,128]{1,0:T(8,128)(2,1)} %slice.12), channel_id=1, source_target_pairs={{0,4},{4,0},{1,5},{5,1},{2,6},{6,2},{3,7},{7,3},{8,12},{12,8},{9,1... | collective-permute-start | bytes 786440 | tf_op jit(solution)/shard_map/ppermute | solution.py:254
  88.5 7.3 %states.4 = (bf16[6,7,128,128]{3,2,1,0:T(8,128)(2,1)}, f32[6,128,128]{2,1,0:T(8,128)}) custom-call(s32[6]{0:T(128)} %get-tuple-element.52.groups_ref, s32[1]{0:T(128)} %bitcast.core_ref.refs_1_, bf16[128,32768]{1,0:T(8,128)(2,1)} %refs_3_.5, f32[2,16,8,256]{3,2,1,0:T(8,128)} %bitcast.30, f32[2,1024,128]{2,1,0:T(8,128)} %get-tuple-element.28.merge_ref, ...), custom_call_target="tpu_custom_call" | custom-call | flops 402653184 | bytes 12582912 | tf_op jit(solution)/shard_map/states/pallas_call | solution.py:386
  95.9 1.8 %collective-permute-done.19 = bf16[2048,128]{1,0:T(8,128)(2,1)S(1)} collective-permute-done((bf16[2048,128]{1,0:T(8,128)(2,1)S(1)}, bf16[2048,128]{1,0:T(8,128)(2,1)S(1)}, u32[]{:S(2)}, u32[]{:S(2)}) %collective-permute-start.19) | collective-permute-done | bytes 524320 | tf_op jit(solution)/shard_map/ppermute | solution.py:254
  97.8 1.1 collective-permute-start.24
  100.8 1.7 collective-permute-start.21
  102.6 0.9 copy-done.5
  103.5 4.7 %states.5 = (bf16[3,7,128,128]{3,2,1,0:T(8,128)(2,1)}, f32[3,128,128]{2,1,0:T(8,128)}) custom-call(s32[3]{0:T(128)} %copy-done.16, s32[1]{0:T(128)} %bitcast.core_ref.refs_1_, bf16[128,32768]{1,0:T(8,128)(2,1)} %refs_3_.5, f32[2,16,8,256]{3,2,1,0:T(8,128)} %bitcast.31, f32[2,1024,128]{2,1,0:T(8,128)} %get-tuple-element.28.merge_ref, ...), custom_call_target="tpu_custom_call" | custom-call | flops 201326592 | bytes 6291456 | tf_op jit(solution)/shard_map/states/pallas_call | solution.py:386
  108.2 3.1 %tree.1.refs_4_ = bf16[16,128,128]{2,1,0:T(8,128)(2,1)} custom-call(s32[16]{0:T(128)} %concatenate.39.groups_ref, f32[2,1024,128]{2,1,0:T(8,128)} %get-tuple-element.28.merge_ref, f32[7,128,128]{2,1,0:T(8,128)} %get-tuple-element.31.refs_0_, f32[6,128,128]{2,1,0:T(8,128)} %get-tuple-element.32.refs_1_, f32[3,128,128]{2,1,0:T(8,128)} %get-tuple-element.38.refs_2_), custom_call_target="tpu_custom_call" | custom-call | tf_op jit(solution)/shard_map/tree/pallas_call | solution.py:496
  111.4 1.0 copy-done
  112.3 12.5 %outputs.3.refs_19_ = bf16[128,32768]{1,0:T(8,128)(2,1)} custom-call(s32[4]{0:T(128)} %pad_add_fusion.2.refs_0_, s32[1]{0:T(128)} %bitcast.core_ref.refs_1_, f32[2]{0:T(128)} %dynamic_slice.3.refs_2_, bf16[128,32768]{1,0:T(8,128)(2,1)} %refs_3_.5, bf16[16,128,128]{2,1,0:T(8,128)(2,1)} %tree.1.refs_4_, f32[2,16,8,256]{3,2,1,0:T(8,128)} %bitcast.23, ...), custom_call_target="tpu_custom_call" | custom-call | flops 2952790016 | bytes 8388608 | tf_op jit(solution)/shard_map/outputs/pallas_call | solution.py:443
  125.4 1.0 collective-permute-start.28
  126.4 1.0 slice.14
  127.8 0.9 copy-done.10
  128.7 20.2 %outputs.4.refs_19_ = bf16[128,32768]{1,0:T(8,128)(2,1)} custom-call(s32[6]{0:T(128)} %get-tuple-element.51.refs_0_, s32[1]{0:T(128)} %bitcast.core_ref.refs_1_, f32[2]{0:T(128)} %dynamic_slice.3.refs_2_, bf16[128,32768]{1,0:T(8,128)(2,1)} %refs_3_.5, bf16[16,128,128]{2,1,0:T(8,128)(2,1)} %tree.1.refs_4_, ...), custom_call_target="tpu_custom_call", output_to_operand_aliasing={{}: (19, {})} | custom-call | flops 4429185024 | bytes 12582912 | tf_op jit(solution)/shard_map/outputs/pallas_call | solution.py:443
  149.3 2.1 %collective-permute-done.29.refs_17_ = bf16[3072,128]{1,0:T(8,128)(2,1)S(1)} collective-permute-done((bf16[3072,128]{1,0:T(8,128)(2,1)S(1)}, bf16[3072,128]{1,0:T(8,128)(2,1)S(1)}, u32[]{:S(2)}, u32[]{:S(2)}) %collective-permute-start.29) | collective-permute-done | bytes 786464 | tf_op jit(solution)/shard_map/ppermute | solution.py:254
  151.4 0.9 copy-done.11
  152.4 22.2 %outputs.5 = bf16[128,32768]{1,0:T(8,128)(2,1)} custom-call(s32[6]{0:T(128)} %get-tuple-element.53.refs_0_, s32[1]{0:T(128)} %bitcast.core_ref.refs_1_, f32[2]{0:T(128)} %dynamic_slice.3.refs_2_, bf16[128,32768]{1,0:T(8,128)(2,1)} %refs_3_.5, bf16[16,128,128]{2,1,0:T(8,128)(2,1)} %tree.1.refs_4_, ...), custom_call_target="tpu_custom_call", output_to_operand_aliasing={{}: (19, {})} | custom-call | flops 4429185024 | bytes 12582912 | tf_op jit(solution)/shard_map/outputs/pallas_call | solution.py:443
  (91 shorter events, 10.9 us)
Async XLA Ops:
  0.0 23.5 %copy-start.12 = (bf16[1024,128]{1,0:T(8,128)(2,1)S(1)}, bf16[1024,128]{1,0:T(8,128)(2,1)}, u32[]{:S(2)}) copy-start(bf16[1024,128]{1,0:T(8,128)(2,1)} %param.8) | copy-start | bytes 786436
  0.0 16.3 %collective-permute-start.5 = (bf16[1024,128]{1,0:T(8,128)(2,1)}, bf16[1024,128]{1,0:T(8,128)(2,1)S(1)}, u32[]{:S(2)}, u32[]{:S(2)}) collective-permute-start(bf16[1024,128]{1,0:T(8,128)(2,1)} %param.8), channel_id=1, source_target_pairs={{0,16},{8,24},{16,0},{24,8},{1,17},{9,25},{17,1},{25,9},{2,18},{10... | collective-permute-start | bytes 786440 | tf_op jit(solution)/shard_map/ppermute | solution.py:254
  4.0 20.2 %collective-permute-start = (bf16[1024,128]{1,0:T(8,128)(2,1)}, bf16[1024,128]{1,0:T(8,128)(2,1)}, u32[]{:S(2)}, u32[]{:S(2)}) collective-permute-start(bf16[1024,128]{1,0:T(8,128)(2,1)} %param.8), channel_id=1, source_target_pairs={{0,2},{2,0},{1,3},{3,1},{4,6},{6,4},{5,7},{7,5},{8,10},{10,8},{9,1... | collective-permute-start | bytes 786440 | tf_op jit(solution)/shard_map/ppermute | solution.py:254
  5.5 21.7 %collective-permute-start.4 = (bf16[1024,128]{1,0:T(8,128)(2,1)}, bf16[1024,128]{1,0:T(8,128)(2,1)S(1)}, u32[]{:S(2)}, u32[]{:S(2)}) collective-permute-start(bf16[1024,128]{1,0:T(8,128)(2,1)} %param.8), channel_id=1, source_target_pairs={{0,8},{8,0},{16,24},{24,16},{1,9},{9,1},{17,25},{25,17},{2,10},{10... | collective-permute-start | bytes 786440 | tf_op jit(solution)/shard_map/ppermute | solution.py:254
  7.1 23.8 %collective-permute-start.1 = (bf16[1024,128]{1,0:T(8,128)(2,1)}, bf16[1024,128]{1,0:T(8,128)(2,1)S(1)}, u32[]{:S(2)}, u32[]{:S(2)}) collective-permute-start(bf16[1024,128]{1,0:T(8,128)(2,1)} %param.8), channel_id=1, source_target_pairs={{0,4},{4,0},{1,5},{5,1},{2,6},{6,2},{3,7},{7,3},{8,12},{12,8},{9,1... | collective-permute-start | bytes 786440 | tf_op jit(solution)/shard_map/ppermute | solution.py:254
  8.6 20.7 %collective-permute-start.8 = (bf16[1024,128]{1,0:T(8,128)(2,1)}, bf16[1024,128]{1,0:T(8,128)(2,1)}, u32[]{:S(2)}, u32[]{:S(2)}) collective-permute-start(bf16[1024,128]{1,0:T(8,128)(2,1)} %param.9), channel_id=1, source_target_pairs={{0,4},{4,0},{1,5},{5,1},{2,6},{6,2},{3,7},{7,3},{8,12},{12,8},{9,1... | collective-permute-start | bytes 786440 | tf_op jit(solution)/shard_map/ppermute | solution.py:254
  10.2 14.0 %copy-start.13 = (bf16[1024,128]{1,0:T(8,128)(2,1)S(1)}, bf16[1024,128]{1,0:T(8,128)(2,1)}, u32[]{:S(2)}) copy-start(bf16[1024,128]{1,0:T(8,128)(2,1)} %param.9) | copy-start | bytes 786436
  16.3 13.6 %collective-permute-start.6 = (bf16[1024,128]{1,0:T(8,128)(2,1)S(1)}, bf16[1024,128]{1,0:T(8,128)(2,1)}, u32[]{:S(2)}, u32[]{:S(2)}) collective-permute-start(bf16[1024,128]{1,0:T(8,128)(2,1)S(1)} %collective-permute-done.5), channel_id=1, source_target_pairs={{0,8},{8,0},{16,24},{24,16},{1,9},{9,1},{17,25},{25,17},{2,10},{10... | collective-permute-start | bytes 786440 | tf_op jit(solution)/shard_map/ppermute | solution.py:254
  17.9 41.7 %all-to-all-start = ((f32[8,4,16,256]{3,2,1,0:T(8,128)}), f32[8,4,16,256]{3,2,1,0:T(8,128)S(1)}, u32[]{:S(2)}, u32[]{:S(2)}) async-start(f32[8,4,16,256]{3,2,1,0:T(8,128)} %bitcast.7), calls=%async_computation | async-start | bytes 1048576 | tf_op jit(solution)/shard_map/all_to_all | solution.py:328
  24.2 8.6 %collective-permute-start.7 = (bf16[1024,128]{1,0:T(8,128)(2,1)S(1)}, bf16[1024,128]{1,0:T(8,128)(2,1)S(1)}, u32[]{:S(2)}, u32[]{:S(2)}) collective-permute-start(bf16[1024,128]{1,0:T(8,128)(2,1)S(1)} %copy-done.13), channel_id=1, source_target_pairs={{0,2},{2,0},{1,3},{3,1},{4,6},{6,4},{5,7},{7,5},{8,10},{10,8},{9,1... | collective-permute-start | bytes 786440 | tf_op jit(solution)/shard_map/ppermute | solution.py:254
  27.3 13.6 %collective-permute-start.2 = (bf16[1024,128]{1,0:T(8,128)(2,1)}, bf16[1024,128]{1,0:T(8,128)(2,1)S(1)}, u32[]{:S(2)}, u32[]{:S(2)}) collective-permute-start(bf16[1024,128]{1,0:T(8,128)(2,1)} %collective-permute-done), channel_id=1, source_target_pairs={{0,4},{4,0},{1,5},{5,1},{2,6},{6,2},{3,7},{7,3},{8,12},{12,8},{9,1... | collective-permute-start | bytes 786440 | tf_op jit(solution)/shard_map/ppermute | solution.py:254
  29.3 13.1 %collective-permute-start.17 = (bf16[1024,128]{1,0:T(8,128)(2,1)}, bf16[1024,128]{1,0:T(8,128)(2,1)S(1)}, u32[]{:S(2)}, u32[]{:S(2)}) collective-permute-start(bf16[1024,128]{1,0:T(8,128)(2,1)} %collective-permute-done.8), channel_id=1, source_target_pairs={{0,2},{2,0},{1,3},{3,1},{4,6},{6,4},{5,7},{7,5},{8,10},{10,8},{9,1... | collective-permute-start | bytes 786440 | tf_op jit(solution)/shard_map/ppermute | solution.py:254
  30.9 28.7 %copy-start.1 = (bf16[3072,128]{1,0:T(8,128)(2,1)}, bf16[3072,128]{1,0:T(8,128)(2,1)S(1)}, u32[]{:S(2)}) copy-start(bf16[3072,128]{1,0:T(8,128)(2,1)S(1)} %pad_maximum_fusion.refs_2_.refs_9_) | copy-start | bytes 2359300
  31.0 1.9 %copy-start.15 = (bf16[1024,128]{1,0:T(8,128)(2,1)}, bf16[1024,128]{1,0:T(8,128)(2,1)S(1)}, u32[]{:S(2)}) copy-start(bf16[1024,128]{1,0:T(8,128)(2,1)S(1)} %collective-permute-done.1) | copy-start | bytes 786436
  32.8 4.0 %copy-start.14 = (bf16[1024,128]{1,0:T(8,128)(2,1)}, bf16[1024,128]{1,0:T(8,128)(2,1)S(1)}, u32[]{:S(2)}) copy-start(bf16[1024,128]{1,0:T(8,128)(2,1)S(1)} %collective-permute-done.7) | copy-start | bytes 786436
  32.8 23.8 %collective-permute-start.12 = (bf16[3072,128]{1,0:T(8,128)(2,1)S(1)}, bf16[3072,128]{1,0:T(8,128)(2,1)S(1)}, u32[]{:S(2)}, u32[]{:S(2)}) collective-permute-start(bf16[3072,128]{1,0:T(8,128)(2,1)S(1)} %pad_maximum_fusion.refs_2_.refs_9_), channel_id=1, source_target_pairs={{0,4},{4,0},{1,5},{5,1},{2,6},{6,2},{3,7},{7,3},{8,12},{12,8},{9,1... | collective-permute-start | bytes 2359304 | tf_op jit(solution)/shard_map/ppermute | solution.py:254
  35.5 21.1 %collective-permute-start.10 = (bf16[3072,128]{1,0:T(8,128)(2,1)S(1)}, bf16[3072,128]{1,0:T(8,128)(2,1)S(1)}, u32[]{:S(2)}, u32[]{:S(2)}) collective-permute-start(bf16[3072,128]{1,0:T(8,128)(2,1)S(1)} %pad_maximum_fusion.refs_2_.refs_9_), channel_id=1, source_target_pairs={{0,2},{2,0},{1,3},{3,1},{4,6},{6,4},{5,7},{7,5},{8,10},{10,8},{9,1... | collective-permute-start | bytes 2359304 | tf_op jit(solution)/shard_map/ppermute | solution.py:254
  38.5 10.8 %collective-permute-start.15 = (bf16[1024,128]{1,0:T(8,128)(2,1)S(1)}, bf16[1024,128]{1,0:T(8,128)(2,1)}, u32[]{:S(2)}, u32[]{:S(2)}) collective-permute-start(bf16[1024,128]{1,0:T(8,128)(2,1)S(1)} %copy-done.13), channel_id=1, source_target_pairs={{0,16},{8,24},{16,0},{24,8},{1,17},{9,25},{17,1},{25,9},{2,18},{10... | collective-permute-start | bytes 786440 | tf_op jit(solution)/shard_map/ppermute | solution.py:254
  41.6 33.9 %collective-permute-start.3 = (bf16[4096,128]{1,0:T(8,128)(2,1)}, bf16[4096,128]{1,0:T(8,128)(2,1)}, u32[]{:S(2)}, u32[]{:S(2)}) collective-permute-start(bf16[4096,128]{1,0:T(8,128)(2,1)} %constant_dynamic-update-slice_fusion.refs_0_.refs_9_), channel_id=1, source_target_pairs={{0,1},{1,0},{2,3},{3,2},{4,5},{5,4},{6,7},{7,6},{8,9},{9,8},{10,11... | collective-permute-start | bytes 3145736 | tf_op jit(solution)/shard_map/ppermute | solution.py:254
  42.4 33.1 %collective-permute-start.9 = (bf16[3072,128]{1,0:T(8,128)(2,1)S(1)}, bf16[3072,128]{1,0:T(8,128)(2,1)}, u32[]{:S(2)}, u32[]{:S(2)}) collective-permute-start(bf16[3072,128]{1,0:T(8,128)(2,1)S(1)} %pad_maximum_fusion.refs_2_.refs_9_), channel_id=1, source_target_pairs={{0,1},{1,0},{2,3},{3,2},{4,5},{5,4},{6,7},{7,6},{8,9},{9,8},{10,11... | collective-permute-start | bytes 2359304 | tf_op jit(solution)/shard_map/ppermute | solution.py:254
  49.3 7.3 %collective-permute-start.14 = (bf16[1024,128]{1,0:T(8,128)(2,1)S(1)}, bf16[1024,128]{1,0:T(8,128)(2,1)}, u32[]{:S(2)}, u32[]{:S(2)}) collective-permute-start(bf16[1024,128]{1,0:T(8,128)(2,1)S(1)} %copy-done.13), channel_id=1, source_target_pairs={{0,8},{8,0},{16,24},{24,16},{1,9},{9,1},{17,25},{25,17},{2,10},{10... | collective-permute-start | bytes 786440 | tf_op jit(solution)/shard_map/ppermute | solution.py:254
  56.6 17.3 %collective-permute-start.16 = (bf16[1024,128]{1,0:T(8,128)(2,1)}, bf16[1024,128]{1,0:T(8,128)(2,1)}, u32[]{:S(2)}, u32[]{:S(2)}) collective-permute-start(bf16[1024,128]{1,0:T(8,128)(2,1)} %collective-permute-done.15), channel_id=1, source_target_pairs={{0,8},{8,0},{16,24},{24,16},{1,9},{9,1},{17,25},{25,17},{2,10},{10... | collective-permute-start | bytes 786440 | tf_op jit(solution)/shard_map/ppermute | solution.py:254
  56.6 28.5 %copy-start.3 = (bf16[3072,128]{1,0:T(8,128)(2,1)}, bf16[3072,128]{1,0:T(8,128)(2,1)S(1)}, u32[]{:S(2)}) copy-start(bf16[3072,128]{1,0:T(8,128)(2,1)S(1)} %collective-permute-done.10.refs_0_.refs_14_) | copy-start | bytes 2359300
  56.6 31.9 %collective-permute-start.11 = (bf16[3072,128]{1,0:T(8,128)(2,1)S(1)}, bf16[3072,128]{1,0:T(8,128)(2,1)}, u32[]{:S(2)}, u32[]{:S(2)}) collective-permute-start(bf16[3072,128]{1,0:T(8,128)(2,1)S(1)} %collective-permute-done.10.refs_0_.refs_14_), channel_id=1, source_target_pairs={{0,1},{1,0},{2,3},{3,2},{4,5},{5,4},{6,7},{7,6},{8,9},{9,8},{10,11... | collective-permute-start | bytes 2359304 | tf_op jit(solution)/shard_map/ppermute | solution.py:254
  56.7 27.2 %copy-start.2 = (bf16[3072,128]{1,0:T(8,128)(2,1)}, bf16[3072,128]{1,0:T(8,128)(2,1)S(1)}, u32[]{:S(2)}) copy-start(bf16[3072,128]{1,0:T(8,128)(2,1)S(1)} %collective-permute-done.12.refs_2_.refs_9_) | copy-start | bytes 2359300
  56.7 31.8 %collective-permute-start.13 = (bf16[3072,128]{1,0:T(8,128)(2,1)S(1)}, bf16[3072,128]{1,0:T(8,128)(2,1)}, u32[]{:S(2)}, u32[]{:S(2)}) collective-permute-start(bf16[3072,128]{1,0:T(8,128)(2,1)S(1)} %collective-permute-done.12.refs_2_.refs_9_), channel_id=1, source_target_pairs={{0,1},{1,0},{2,3},{3,2},{4,5},{5,4},{6,7},{7,6},{8,9},{9,8},{10,11... | collective-permute-start | bytes 2359304 | tf_op jit(solution)/shard_map/ppermute | solution.py:254
  59.6 2.9 %copy-start.7 = (f32[8,4,16,256]{3,2,1,0:T(8,128)}, f32[8,4,16,256]{3,2,1,0:T(8,128)S(1)}, u32[]{:S(2)}) copy-start(f32[8,4,16,256]{3,2,1,0:T(8,128)S(1)} %all-to-all-done.gates_ref) | copy-start | bytes 1572868
  62.5 48.9 %all-to-all-start.1 = ((bf16[8,16,4096]{2,1,0:T(8,128)(2,1)}), bf16[8,16,4096]{2,1,0:T(8,128)(2,1)S(1)}, u32[]{:S(2)}, u32[]{:S(2)}) async-start(bf16[8,16,4096]{2,1,0:T(8,128)(2,1)} %bitcast.22), calls=%async_computation.1 | async-start | bytes 2097152 | tf_op jit(solution)/shard_map/all_to_all | solution.py:361
  83.9 13.8 %collective-permute-start.19 = (bf16[2048,128]{1,0:T(8,128)(2,1)S(1)}, bf16[2048,128]{1,0:T(8,128)(2,1)S(1)}, u32[]{:S(2)}, u32[]{:S(2)}) collective-permute-start(bf16[2048,128]{1,0:T(8,128)(2,1)S(1)} %slice.13), channel_id=1, source_target_pairs={{0,2},{2,0},{1,3},{3,1},{4,6},{6,4},{5,7},{7,5},{8,10},{10,8},{9,1... | collective-permute-start | bytes 1572872 | tf_op jit(solution)/shard_map/ppermute | solution.py:254
  85.8 10.0 %collective-permute-start.18 = (bf16[1024,128]{1,0:T(8,128)(2,1)}, bf16[1024,128]{1,0:T(8,128)(2,1)S(1)}, u32[]{:S(2)}, u32[]{:S(2)}) collective-permute-start(bf16[1024,128]{1,0:T(8,128)(2,1)} %slice.12), channel_id=1, source_target_pairs={{0,4},{4,0},{1,5},{5,1},{2,6},{6,2},{3,7},{7,3},{8,12},{12,8},{9,1... | collective-permute-start | bytes 786440 | tf_op jit(solution)/shard_map/ppermute | solution.py:254
  87.8 11.2 %copy-start.16 = (s32[3]{0:T(128)}, s32[3]{0:T(128)S(1)}, u32[]{:S(2)}) copy-start(s32[3]{0:T(128)S(1)} %get-tuple-element.57.groups_ref) | copy-start | bytes 40
  88.5 22.9 %collective-permute-start.22 = (bf16[4096,128]{1,0:T(8,128)(2,1)}, bf16[4096,128]{1,0:T(8,128)(2,1)}, u32[]{:S(2)}, u32[]{:S(2)}) collective-permute-start(bf16[4096,128]{1,0:T(8,128)(2,1)} %constant_dynamic-update-slice_fusion.7.refs_11_), channel_id=1, source_target_pairs={{0,1},{1,0},{2,3},{3,2},{4,5},{5,4},{6,7},{7,6},{8,9},{9,8},{10,11... | collective-permute-start | bytes 3145736 | tf_op jit(solution)/shard_map/ppermute | solution.py:254
  95.8 3.8 %copy-start.17 = (f32[16]{0:T(128)S(1)}, f32[16]{0:T(128)}, u32[]{:S(2)}) copy-start(f32[16]{0:T(128)} %param.13) | copy-start | bytes 196
  97.8 4.8 %copy-start.4 = (bf16[3072,128]{1,0:T(8,128)(2,1)}, bf16[3072,128]{1,0:T(8,128)(2,1)S(1)}, u32[]{:S(2)}) copy-start(bf16[3072,128]{1,0:T(8,128)(2,1)S(1)} %constant_dynamic-update-slice_fusion.11.refs_0_.refs_14_) | copy-start | bytes 2359300
  97.8 4.8 %collective-permute-start.20 = (bf16[3072,128]{1,0:T(8,128)(2,1)S(1)}, bf16[3072,128]{1,0:T(8,128)(2,1)S(1)}, u32[]{:S(2)}, u32[]{:S(2)}) collective-permute-start(bf16[3072,128]{1,0:T(8,128)(2,1)S(1)} %constant_dynamic-update-slice_fusion.11.refs_0_.refs_14_), channel_id=1, source_target_pairs={{0,1},{1,0},{2,3},{3,2},{4,5},{5,4},{6,7},{7,6},{8,9},{9,8},{10,11... | collective-permute-start | bytes 2359304 | tf_op jit(solution)/shard_map/ppermute | solution.py:254
  97.8 26.9 %collective-permute-start.24 = (bf16[3072,128]{1,0:T(8,128)(2,1)}, bf16[3072,128]{1,0:T(8,128)(2,1)}, u32[]{:S(2)}, u32[]{:S(2)}) collective-permute-start(bf16[3072,128]{1,0:T(8,128)(2,1)} %constant_dynamic-update-slice_fusion.4.refs_11_), channel_id=1, source_target_pairs={{0,2},{2,0},{1,3},{3,1},{4,6},{6,4},{5,7},{7,5},{8,10},{10,8},{9,1... | collective-permute-start | bytes 2359304 | tf_op jit(solution)/shard_map/ppermute | solution.py:254
  100.8 24.5 %collective-permute-start.21 = (bf16[3072,128]{1,0:T(8,128)(2,1)}, bf16[3072,128]{1,0:T(8,128)(2,1)S(1)}, u32[]{:S(2)}, u32[]{:S(2)}) collective-permute-start(bf16[3072,128]{1,0:T(8,128)(2,1)} %constant_dynamic-update-slice_fusion.4.refs_11_), channel_id=1, source_target_pairs={{0,4},{4,0},{1,5},{5,1},{2,6},{6,2},{3,7},{7,3},{8,12},{12,8},{9,1... | collective-permute-start | bytes 2359304 | tf_op jit(solution)/shard_map/ppermute | solution.py:254
  102.6 25.2 %collective-permute-start.26 = (bf16[3072,128]{1,0:T(8,128)(2,1)}, bf16[3072,128]{1,0:T(8,128)(2,1)}, u32[]{:S(2)}, u32[]{:S(2)}) collective-permute-start(bf16[3072,128]{1,0:T(8,128)(2,1)} %constant_dynamic-update-slice_fusion.4.refs_11_), channel_id=1, source_target_pairs={{0,1},{1,0},{2,3},{3,2},{4,5},{5,4},{6,7},{7,6},{8,9},{9,8},{10,11... | collective-permute-start | bytes 2359304 | tf_op jit(solution)/shard_map/ppermute | solution.py:254
  111.4 1.0 copy-start
  124.8 3.0 %collective-permute-start.27 = (bf16[3072,128]{1,0:T(8,128)(2,1)}, bf16[3072,128]{1,0:T(8,128)(2,1)S(1)}, u32[]{:S(2)}, u32[]{:S(2)}) collective-permute-start(bf16[3072,128]{1,0:T(8,128)(2,1)} %collective-permute-done.24.refs_16_), channel_id=1, source_target_pairs={{0,1},{1,0},{2,3},{3,2},{4,5},{5,4},{6,7},{7,6},{8,9},{9,8},{10,11... | collective-permute-start | bytes 2359304 | tf_op jit(solution)/shard_map/ppermute | solution.py:254
  125.4 23.6 %copy-start.6 = (bf16[3072,128]{1,0:T(8,128)(2,1)}, bf16[3072,128]{1,0:T(8,128)(2,1)S(1)}, u32[]{:S(2)}) copy-start(bf16[3072,128]{1,0:T(8,128)(2,1)S(1)} %collective-permute-done.21.refs_11_) | copy-start | bytes 2359300
  125.4 23.5 %collective-permute-start.28 = (bf16[2048,128]{1,0:T(8,128)(2,1)S(1)}, bf16[2048,128]{1,0:T(8,128)(2,1)S(1)}, u32[]{:S(2)}, u32[]{:S(2)}) collective-permute-start(bf16[2048,128]{1,0:T(8,128)(2,1)S(1)} %slice.15), channel_id=1, source_target_pairs={{0,2},{2,0},{1,3},{3,1},{4,6},{6,4},{5,7},{7,5},{8,10},{10,8},{9,1... | collective-permute-start | bytes 1572872 | tf_op jit(solution)/shard_map/ppermute | solution.py:254
  127.4 21.9 %collective-permute-start.23 = (bf16[3072,128]{1,0:T(8,128)(2,1)S(1)}, bf16[3072,128]{1,0:T(8,128)(2,1)S(1)}, u32[]{:S(2)}, u32[]{:S(2)}) collective-permute-start(bf16[3072,128]{1,0:T(8,128)(2,1)S(1)} %collective-permute-done.21.refs_11_), channel_id=1, source_target_pairs={{0,1},{1,0},{2,3},{3,2},{4,5},{5,4},{6,7},{7,6},{8,9},{9,8},{10,11... | collective-permute-start | bytes 2359304 | tf_op jit(solution)/shard_map/ppermute | solution.py:254
  127.5 21.5 %collective-permute-start.25 = (bf16[1024,128]{1,0:T(8,128)(2,1)S(1)}, bf16[1024,128]{1,0:T(8,128)(2,1)S(1)}, u32[]{:S(2)}, u32[]{:S(2)}) collective-permute-start(bf16[1024,128]{1,0:T(8,128)(2,1)S(1)} %slice.14), channel_id=1, source_target_pairs={{0,4},{4,0},{1,5},{5,1},{2,6},{6,2},{3,7},{7,3},{8,12},{12,8},{9,1... | collective-permute-start | bytes 786440 | tf_op jit(solution)/shard_map/ppermute | solution.py:254
  149.1 2.4 %copy-start.8 = (bf16[3072,128]{1,0:T(8,128)(2,1)}, bf16[3072,128]{1,0:T(8,128)(2,1)S(1)}, u32[]{:S(2)}) copy-start(bf16[3072,128]{1,0:T(8,128)(2,1)S(1)} %constant_dynamic-update-slice_fusion.13.refs_16_) | copy-start | bytes 2359300
  149.1 2.4 %collective-permute-start.29 = (bf16[3072,128]{1,0:T(8,128)(2,1)S(1)}, bf16[3072,128]{1,0:T(8,128)(2,1)S(1)}, u32[]{:S(2)}, u32[]{:S(2)}) collective-permute-start(bf16[3072,128]{1,0:T(8,128)(2,1)S(1)} %constant_dynamic-update-slice_fusion.13.refs_16_), channel_id=1, source_target_pairs={{0,1},{1,0},{2,3},{3,2},{4,5},{5,4},{6,7},{7,6},{8,9},{9,8},{10,11... | collective-permute-start | bytes 2359304 | tf_op jit(solution)/shard_map/ppermute | solution.py:254
  149.3 2.1 %copy-start.9 = (bf16[3072,128]{1,0:T(8,128)(2,1)}, bf16[3072,128]{1,0:T(8,128)(2,1)S(1)}, u32[]{:S(2)}) copy-start(bf16[3072,128]{1,0:T(8,128)(2,1)S(1)} %collective-permute-done.23.refs_12_) | copy-start | bytes 2359300
  151.4 0.9 copy-start.11
  (2 other events, 1.8 us)
